TPU v7x, 256 devices: a whole 4x4x8 slice. The times are simulated.
256 devices in a mesh: seq: 16 (over z_lo, y), ch: 8 (over x, core), batch: 2 (over z_hi).
Axes of the slice: x: 4, y: 4, z: 8 (z_hi: 2, z_lo: 4; z = z_hi * 4 + z_lo), core: 2. Of those that a mesh axis runs over, the one named last changes fastest.
Arguments:
- query_gate: bfloat16 [2, 16384, 2048], P('batch', ('seq', 'ch')), may hold values from -6 to 6
- key_gate: bfloat16 [2, 16384, 2048], P('batch', ('seq', 'ch')), may hold values from -6 to 6
- value_input: bfloat16 [2, 16384, 2048], P('batch', ('seq', 'ch')), may hold values from -6 to 6
- long_filter: bfloat16 [16384, 2048], P('seq', 'ch'), may hold values from -0.046875 to 0.046875
- skip_gain: float32 [2048], replicated, may hold values from -4 to 4
Outputs:
- gated: bfloat16 [2, 16384, 2048], P('batch', ('seq', 'ch'))
All inputs are finite; a program needn't handle non-finite values.
Results may differ from a plain program's by a relative error of at most 0.0053.
Values may be sent and summed in bfloat16 or wider, within the bound.
No kernel may reach another device: no remote copies, remote signals or barrier semaphores. Data moves between devices by JAX's collectives and lax.ppermute only.
A program may use at most 128 MiB of HBM per device.

v0:
```python
import math

import jax
import jax.numpy as jnp
from jax import lax
from jax.sharding import PartitionSpec as P

HIGHEST = lax.Precision.HIGHEST


def unit_roots(rows_idx, cols_idx, modulus):
    products = rows_idx[:, None] * cols_idx[None, :] % modulus
    angles = products.astype(jnp.float32) * (2.0 * math.pi / modulus)
    return (jnp.cos(angles), jnp.sin(angles))


def ccontract(form, cos_tab, sin_tab, sense, pair):
    table = jnp.stack(
        [jnp.stack([cos_tab, sense * sin_tab]), jnp.stack([-sense * sin_tab, cos_tab])]
    )
    return jnp.einsum(form, table, pair, precision=HIGHEST, preferred_element_type=jnp.float32)


def rotate(pair, cos_tab, sin_tab, sense):
    real_part = pair[0]
    imag_part = pair[1]
    return jnp.stack(
        [
            real_part * cos_tab + sense * imag_part * sin_tab,
            imag_part * cos_tab - sense * real_part * sin_tab,
        ]
    )


def real_start(form, cos_tab, sin_tab, operand):
    table = jnp.stack([cos_tab, -sin_tab])
    return jnp.einsum(form, table, operand, precision=HIGHEST, preferred_element_type=jnp.float32)


def factor_pair(length):
    divisor = 1
    for factor in range(1, length + 1):
        if factor * factor > length:
            break
        if length % factor == 0:
            divisor = factor
    return (divisor, length // divisor)


def forward_local(pair):
    leading = pair.shape[1:-2]
    length = pair.shape[-2]
    channel_count = pair.shape[-1]
    outer_size, inner_size = factor_pair(length)
    pair = pair.reshape((2,) + leading + (outer_size, inner_size, channel_count))
    outer_idx = jnp.arange(outer_size, dtype=jnp.int32)
    inner_idx = jnp.arange(inner_size, dtype=jnp.int32)
    one_cos, one_sin = unit_roots(outer_idx, outer_idx, outer_size)
    step = ccontract("xyka,y...abc->x...kbc", one_cos, one_sin, 1.0, pair)
    tw_cos, tw_sin = unit_roots(outer_idx, inner_idx, length)
    turned = rotate(step, tw_cos[:, :, None], tw_sin[:, :, None], 1.0)
    two_cos, two_sin = unit_roots(inner_idx, inner_idx, inner_size)
    return ccontract("xylb,y...kbc->x...klc", two_cos, two_sin, 1.0, turned)


def inverse_local(pair):
    leading = pair.shape[1:-3]
    outer_size = pair.shape[-3]
    inner_size = pair.shape[-2]
    channel_count = pair.shape[-1]
    length = outer_size * inner_size
    outer_idx = jnp.arange(outer_size, dtype=jnp.int32)
    inner_idx = jnp.arange(inner_size, dtype=jnp.int32)
    two_cos, two_sin = unit_roots(inner_idx, inner_idx, inner_size)
    step = ccontract("xylb,y...klc->x...kbc", two_cos, two_sin, -1.0, pair)
    tw_cos, tw_sin = unit_roots(outer_idx, inner_idx, length)
    turned = rotate(step, tw_cos[:, :, None], tw_sin[:, :, None], -1.0)
    one_cos, one_sin = unit_roots(outer_idx, outer_idx, outer_size)
    done = ccontract("xyka,y...kbc->x...abc", one_cos, one_sin, -1.0, turned)
    return done.reshape((2,) + leading + (length, channel_count))


def spectral_product(spec):
    return jnp.stack(
        [
            spec[0, 0] * spec[0, 1] - spec[1, 0] * spec[1, 1],
            spec[0, 0] * spec[1, 1] + spec[1, 0] * spec[0, 1],
        ]
    )


def body(query_gate, key_gate, value_input, long_filter, skip_gain):
    mixed_in = (key_gate[0].astype(jnp.float32) * value_input[0].astype(jnp.float32)).astype(
        jnp.bfloat16
    )
    conv_in = lax.all_to_all(mixed_in, "ch", split_axis=1, concat_axis=0, tiled=True)
    blocks = lax.axis_size("seq")
    doubled = 2 * blocks
    length = conv_in.shape[0]
    padded_len = doubled * length
    seq_pos = lax.axis_index("seq")
    per_device = doubled // blocks
    slice_len = length // blocks
    parts = (
        lax.all_to_all(conv_in[None], "seq", split_axis=1, concat_axis=0, tiled=True),
        lax.all_to_all(long_filter[None], "seq", split_axis=1, concat_axis=0, tiled=True),
    )
    stacked = jnp.stack(parts).astype(jnp.float32)
    block_idx = jnp.arange(blocks, dtype=jnp.int32)
    freq_idx = jnp.arange(doubled, dtype=jnp.int32)
    s_cos, s_sin = unit_roots(freq_idx, block_idx, doubled)
    pair = real_start("xks,zsqc->xzkqc", s_cos, s_sin, stacked)
    positions = seq_pos * slice_len + jnp.arange(slice_len, dtype=jnp.int32)
    t_cos, t_sin = unit_roots(freq_idx, positions, padded_len)
    turned = rotate(pair, t_cos[:, :, None], t_sin[:, :, None], 1.0)
    packed = turned.reshape((4,) + turned.shape[2:])
    packet = lax.all_to_all(packed, "seq", split_axis=1, concat_axis=2, tiled=True)
    spec = forward_local(packet.reshape((2, 2) + packet.shape[1:]))
    back = inverse_local(spectral_product(spec))
    freq_rows = seq_pos * per_device + jnp.arange(per_device, dtype=jnp.int32)
    c_cos, c_sin = unit_roots(freq_rows, jnp.arange(length, dtype=jnp.int32), padded_len)
    unrotated = rotate(back, c_cos[:, :, None], c_sin[:, :, None], -1.0)
    collected = lax.all_to_all(unrotated, "seq", split_axis=2, concat_axis=1, tiled=True)
    i_cos, i_sin = unit_roots(block_idx, freq_idx, doubled)
    table = jnp.stack([i_cos, -i_sin])
    result = jnp.einsum(
        "xsk,xkqc->sqc", table, collected, precision=HIGHEST, preferred_element_type=jnp.float32
    )
    result = (result * (1.0 / padded_len)).astype(jnp.bfloat16)
    conv_rows = lax.all_to_all(
        lax.all_to_all(result, "seq", split_axis=0, concat_axis=1, tiled=True),
        "ch",
        split_axis=1,
        concat_axis=2,
        tiled=True,
    )[0]
    direct = lax.optimization_barrier(mixed_in).astype(jnp.float32)
    joined = conv_rows.astype(jnp.float32) + skip_gain[None, :] * direct
    return (query_gate[0].astype(jnp.float32) * joined).astype(jnp.bfloat16)[None]


def solution(mesh):
    return jax.shard_map(
        body,
        mesh=mesh,
        in_specs=(
            P("batch", ("seq", "ch"), None),
            P("batch", ("seq", "ch"), None),
            P("batch", ("seq", "ch"), None),
            P("seq", "ch"),
            P(),
        ),
        out_specs=P("batch", ("seq", "ch"), None),
        check_vma=False,
    )
```

profile of v0, /device:TPU:1, one launch (start us, length us, event | category | flops | bytes accessed | tf_op | source)
XLA Modules:
  0.0 481.6 jit_solution(14863059613575433992)
XLA Ops:
  3.7 6.6 %all-to-all-start = ((bf16[128,8,256]{0,2,1:T(8,128)(2,1)}), bf16[128,8,256]{0,2,1:T(8,128)(2,1)S(1)}, u32[]{:S(2)}, u32[]{:S(2)}) async-start(bf16[128,8,256]{0,2,1:T(8,128)(2,1)} %bitcast.2), calls=%async_computation | async-start | bytes 1048576 | tf_op jit(solution)/shard_map/all_to_all | solution.py:96
  19.8 7.5 %all-to-all-start.2 = ((bf16[16,2,8192]{2,1,0:T(2,128)(2,1)}), bf16[16,2,8192]{2,1,0:T(2,128)(2,1)S(1)}, u32[]{:S(2)}, u32[]{:S(2)}) async-start(bf16[16,2,8192]{2,1,0:T(2,128)(2,1)} %reshape.599), calls=%async_computation.2 | async-start | bytes 1048576 | tf_op jit(solution)/shard_map/all_to_all | solution.py:106
  28.3 3.8 reduce.1
  33.1 7.9 %all-to-all-done.2 = bf16[16,2,8192]{2,1,0:T(2,128)(2,1)S(1)} async-done(((bf16[16,2,8192]{2,1,0:T(2,128)(2,1)}), bf16[16,2,8192]{2,1,0:T(2,128)(2,1)S(1)}, u32[]{:S(2)}, u32[]{:S(2)}) %all-to-all-start.2) | async-done | bytes 524320 | tf_op jit(solution)/shard_map/all_to_all | solution.py:106
  41.0 5.5 %all-to-all-start.1 = ((bf16[16,2,8192]{2,1,0:T(2,128)(2,1)}), bf16[16,2,8192]{2,1,0:T(2,128)(2,1)S(1)}, u32[]{:S(2)}, u32[]{:S(2)}) async-start(bf16[16,2,8192]{2,1,0:T(2,128)(2,1)} %reshape.601), calls=%async_computation.1 | async-start | bytes 1048576 | tf_op jit(solution)/shard_map/all_to_all | solution.py:105
  47.7 11.9 %all-to-all-done.1 = bf16[16,2,8192]{2,1,0:T(2,128)(2,1)S(1)} async-done(((bf16[16,2,8192]{2,1,0:T(2,128)(2,1)}), bf16[16,2,8192]{2,1,0:T(2,128)(2,1)S(1)}, u32[]{:S(2)}, u32[]{:S(2)}) %all-to-all-start.1) | async-done | bytes 524320 | tf_op jit(solution)/shard_map/all_to_all | solution.py:105
  66.8 4.9 %copy.110 = f32[2,2,32,64,256]{4,3,2,1,0:T(8,128)S(1)} copy(f32[2,2,32,64,256]{4,2,0,3,1:T(8,128)S(1)} %pad_maximum_fusion) | data formatting | bytes 16777216 | tf_op jit(solution)/shard_map/stack | solution.py:27
  71.7 3.9 copy.111
  75.6 6.0 %all-to-all-start.3 = ((f32[4,32,64,256]{3,2,0,1:T(8,128)}), f32[4,32,64,256]{3,2,0,1:T(8,128)}, u32[]{:S(2)}, u32[]{:S(2)}) async-start(f32[4,32,64,256]{3,2,0,1:T(8,128)} %copy.111), calls=%async_computation.3 | async-start | bytes 16777216 | tf_op jit(solution)/shard_map/all_to_all | solution.py:117
  82.3 150.1 %all-to-all-done.3 = f32[4,32,64,256]{3,2,0,1:T(8,128)} async-done(((f32[4,32,64,256]{3,2,0,1:T(8,128)}), f32[4,32,64,256]{3,2,0,1:T(8,128)}, u32[]{:S(2)}, u32[]{:S(2)}) %all-to-all-start.3) | async-done | bytes 8388640 | tf_op jit(solution)/shard_map/all_to_all | solution.py:117
  232.4 4.0 copy.113
  236.4 13.0 %fusion.8 = f32[2,2,2,32,32,256]{5,3,0,4,2,1:T(8,128)S(1)} fusion(f32[2,2,2,32,32,256,1]{5,4,3,2,1,0,6:T(8,128)S(1)} %bitcast.161, f32[1,2,32,32]{3,2,1,0:T(8,128)S(1)} %get-tuple-element.16, f32[1,2,32,32]{3,2,1,0:T(8,128)S(1)} %get-tuple-element.19), kind=kOutput, calls=%fused_computation.18 | convolution fusion | flops 1610616832 | bytes 16793600 | tf_op jit(solution)/shard_map/xyka,y...abc->x...kbc/dot_general | solution.py:21
  252.3 13.8 %fusion.11 = f32[2,2,2,32,32,256]{5,4,0,3,2,1:T(8,128)S(1)} fusion(f32[2,2,2,32,32,256,1]{5,3,0,4,2,1,6:T(8,128)S(1)} %maximum_bitcast_fusion, f32[1,2,32,32]{3,2,1,0:T(8,128)S(1)} %get-tuple-element.16, f32[1,2,32,32]{3,2,1,0:T(8,128)S(1)} %get-tuple-element.19), kind=kOutput, calls=%fused_computation.19 | convolution fusion | flops 1610616832 | bytes 16793600 | tf_op jit(solution)/shard_map/xylb,y...kbc->x...klc/dot_general | solution.py:21
  268.5 4.0 fusion.14
  273.6 6.6 %fusion.17 = f32[2,2,32,32,256]{4,2,0,3,1:T(8,128)S(1)} fusion(f32[2,2,32,32,256,1]{4,3,0,2,1,5:T(8,128)S(1)} %maximum_bitcast_fusion.2, f32[1,2,32,32]{3,2,1,0:T(8,128)S(1)} %get-tuple-element.20, f32[1,2,32,32]{3,2,1,0:T(8,128)S(1)} %get-tuple-element.15), kind=kOutput, calls=%fused_computation.21 | convolution fusion | flops 805310464 | bytes 8404992 | tf_op jit(solution)/shard_map/xyka,y...kbc->x...abc/dot_general | solution.py:21
  284.7 5.2 %copy.130 = f32[2,2,1024,256]{3,1,0,2:T(2,128)} copy(f32[2,2,1024,256]{3,2,1,0:T(8,128)S(1)} %pad_maximum_fusion.1) | data formatting | bytes 8388608 | tf_op jit(solution)/shard_map/stack | solution.py:27
  289.9 36.5 %all-to-all-start.4 = ((f32[2,2,1024,256]{3,1,0,2:T(2,128)}), f32[2,2,1024,256]{3,1,0,2:T(2,128)}, u32[]{:S(2)}, u32[]{:S(2)}) async-start(f32[2,2,1024,256]{3,1,0,2:T(2,128)} %copy.130), calls=%async_computation.4 | async-start | bytes 8388608 | tf_op jit(solution)/shard_map/all_to_all | solution.py:123
  326.5 78.1 %all-to-all-done.4 = f32[2,2,1024,256]{3,1,0,2:T(2,128)} async-done(((f32[2,2,1024,256]{3,1,0,2:T(2,128)}), f32[2,2,1024,256]{3,1,0,2:T(2,128)}, u32[]{:S(2)}, u32[]{:S(2)}) %all-to-all-start.4) | async-done | bytes 4194336 | tf_op jit(solution)/shard_map/all_to_all | solution.py:123
  407.6 5.2 %copy.132 = f32[2,16,2,64,256]{4,2,1,0,3:T(2,128)} copy(f32[2,16,2,64,256]{4,3,1,2,0:T(8,128)S(1)} %bitcast.162) | data formatting | bytes 8388608 | tf_op jit(solution)/shard_map/all_to_all | solution.py:123
  412.8 6.1 %all_to_all.80 = f32[2,32,64,256]{3,1,0,2:T(8,128)} reshape(f32[2,16,2,64,256]{4,2,1,0,3:T(2,128)} %copy.132) | data formatting | bytes 8388608 | tf_op jit(solution)/shard_map/all_to_all | solution.py:123
  418.9 4.3 fusion.26
  423.4 32.6 %all_to_all.91 = bf16[16,64,256]{2,1,0:T(8,128)(2,1)S(1)} all-to-all(bf16[16,64,256]{2,1,0:T(8,128)(2,1)S(1)} %copy.133), channel_id=1, replica_groups=mesh['seq'=16,'ch'=8,'batch'=2] {'seq'}, dimensions={0} | all-to-all | bytes 1048576 | tf_op jit(solution)/shard_map/all_to_all | solution.py:131
  461.5 6.7 %all-to-all-start.6 = ((bf16[8,2,16384]{2,1,0:T(2,128)(2,1)}), bf16[8,2,16384]{2,1,0:T(2,128)(2,1)S(1)}, u32[]{:S(2)}, u32[]{:S(2)}) async-start(bf16[8,2,16384]{2,1,0:T(2,128)(2,1)} %reshape.603), calls=%async_computation.6 | async-start | bytes 1048576 | tf_op jit(solution)/shard_map/all_to_all | solution.py:130
  468.5 9.2 %all-to-all-done.6 = bf16[8,2,16384]{2,1,0:T(2,128)(2,1)S(1)} async-done(((bf16[8,2,16384]{2,1,0:T(2,128)(2,1)}), bf16[8,2,16384]{2,1,0:T(2,128)(2,1)S(1)}, u32[]{:S(2)}, u32[]{:S(2)}) %all-to-all-start.6) | async-done | bytes 524320 | tf_op jit(solution)/shard_map/all_to_all | solution.py:130
  (62 shorter events, 47.5 us)
Async XLA Ops:
  0.0 10.3 %copy-start = (bf16[1024,256]{1,0:T(8,128)(2,1)S(1)}, bf16[1024,256]{1,0:T(8,128)(2,1)}, u32[]{:S(2)}) copy-start(bf16[1024,256]{1,0:T(8,128)(2,1)} %param.8) | copy-start | bytes 1572868
  3.7 16.1 %all-to-all-start = ((bf16[128,8,256]{0,2,1:T(8,128)(2,1)}), bf16[128,8,256]{0,2,1:T(8,128)(2,1)S(1)}, u32[]{:S(2)}, u32[]{:S(2)}) async-start(bf16[128,8,256]{0,2,1:T(8,128)(2,1)} %bitcast.2), calls=%async_computation | async-start | bytes 1048576 | tf_op jit(solution)/shard_map/all_to_all | solution.py:96
  19.8 21.2 %all-to-all-start.2 = ((bf16[16,2,8192]{2,1,0:T(2,128)(2,1)}), bf16[16,2,8192]{2,1,0:T(2,128)(2,1)S(1)}, u32[]{:S(2)}, u32[]{:S(2)}) async-start(bf16[16,2,8192]{2,1,0:T(2,128)(2,1)} %reshape.599), calls=%async_computation.2 | async-start | bytes 1048576 | tf_op jit(solution)/shard_map/all_to_all | solution.py:106
  41.0 18.6 %all-to-all-start.1 = ((bf16[16,2,8192]{2,1,0:T(2,128)(2,1)}), bf16[16,2,8192]{2,1,0:T(2,128)(2,1)S(1)}, u32[]{:S(2)}, u32[]{:S(2)}) async-start(bf16[16,2,8192]{2,1,0:T(2,128)(2,1)} %reshape.601), calls=%async_computation.1 | async-start | bytes 1048576 | tf_op jit(solution)/shard_map/all_to_all | solution.py:105
  75.6 156.8 %all-to-all-start.3 = ((f32[4,32,64,256]{3,2,0,1:T(8,128)}), f32[4,32,64,256]{3,2,0,1:T(8,128)}, u32[]{:S(2)}, u32[]{:S(2)}) async-start(f32[4,32,64,256]{3,2,0,1:T(8,128)} %copy.111), calls=%async_computation.3 | async-start | bytes 16777216 | tf_op jit(solution)/shard_map/all_to_all | solution.py:117
  289.9 114.7 %all-to-all-start.4 = ((f32[2,2,1024,256]{3,1,0,2:T(2,128)}), f32[2,2,1024,256]{3,1,0,2:T(2,128)}, u32[]{:S(2)}, u32[]{:S(2)}) async-start(f32[2,2,1024,256]{3,1,0,2:T(2,128)} %copy.130), calls=%async_computation.4 | async-start | bytes 8388608 | tf_op jit(solution)/shard_map/all_to_all | solution.py:123
  423.2 45.1 %copy-start.1 = (bf16[1,128,2048]{2,1,0:T(8,128)(2,1)S(1)}, bf16[1,128,2048]{2,1,0:T(8,128)(2,1)}, u32[]{:S(2)}) copy-start(bf16[1,128,2048]{2,1,0:T(8,128)(2,1)} %param.5) | copy-start | bytes 1572868
  461.5 16.2 %all-to-all-start.6 = ((bf16[8,2,16384]{2,1,0:T(2,128)(2,1)}), bf16[8,2,16384]{2,1,0:T(2,128)(2,1)S(1)}, u32[]{:S(2)}, u32[]{:S(2)}) async-start(bf16[8,2,16384]{2,1,0:T(2,128)(2,1)} %reshape.603), calls=%async_computation.6 | async-start | bytes 1048576 | tf_op jit(solution)/shard_map/all_to_all | solution.py:130
  468.2 10.6 %copy-start.2 = (f32[2048]{0:T(1024)S(1)}, f32[2048]{0:T(1024)}, u32[]{:S(2)}) copy-start(f32[2048]{0:T(1024)} %param.9) | copy-start | bytes 24580
where the time goes:
time: 490 us; the launch traced here: 482 us
  waiting for transfers between devices  261 us (53%)
  starting transfers between devices  68.8 us (14%)
  local copies, waits for them, and re-layouts  48.2 us (10%)
  matrix products  45.2 us (9%)
  blocking collectives  32.6 us (7%)
  other arithmetic  25.4 us (5%)
    all_to_all x1, waiting for transfers between devices, body(): lax.all_to_all(packed, 'seq', split_axis=1, concat_axis=2, tiled=True)  150 us
    all_to_all x1, waiting for transfers between devices, body(): lax.all_to_all(unrotated, 'seq', split_axis=2, concat_axis=1, tiled=True)  78.1 us
    dot_general x4, matrix products, ccontract(): jnp.einsum(form, table, pair, precision=HIGHEST, preferred_element_type=j...  37.5 us
    all_to_all x1, starting transfers between devices, body(): lax.all_to_all(unrotated, 'seq', split_axis=2, concat_axis=1, tiled=True)  36.5 us
    all_to_all x1, blocking collectives, body(): lax.all_to_all(result, 'seq', split_axis=0, concat_axis=1, tiled=True)  32.6 us
    all_to_all x3, local copies, waits for them, and re-layouts, body(): lax.all_to_all(unrotated, 'seq', split_axis=2, concat_axis=1, tiled=True)  14.3 us
    all_to_all x1, waiting for transfers between devices, body(): lax.all_to_all(conv_in[None], 'seq', split_axis=1, concat_axis=0, tiled=T...  11.9 us
    unnamed x3, other arithmetic  11.4 us
  transfers between devices with their start and end apart: 6, of which 6 were waited for; matrix products, arithmetic and copies ran while one was open for 3% of the time, Pallas kernels for 0%

commit v1 on v0

v1 whole, which is shorter than its diff:
```python
import jax
import jax.numpy as jnp
from jax import lax
from jax.experimental import pallas as pl
from jax.experimental.pallas import tpu as pltpu
from jax.sharding import PartitionSpec as P

F32 = jnp.float32
BF = jnp.bfloat16
ALL = ("batch", "seq", "ch")
VM = pl.BlockSpec(memory_space=pltpu.VMEM)


def mix_kernel(k_ref, v_ref, o_ref):
    for ch in range(8):
        cols = slice(ch * 256, (ch + 1) * 256)
        mixed = (k_ref[:, cols].astype(F32) * v_ref[:, cols].astype(F32)).astype(BF)
        turned = mixed.astype(F32).T.reshape(16, 2, 8, 128).astype(BF)
        for b in range(2):
            o_ref[b, :, ch] = turned[:, b]


def filter_kernel(b_ref, f_ref, o_ref):
    turned = f_ref[...].astype(F32).T.reshape(16, 2, 8, 1024)
    o_ref[...] = jnp.where(b_ref[0] == 0, turned[:, 0], turned[:, 1]).astype(BF)


def gate_kernel(c_ref, q_ref, k_ref, v_ref, s_ref, o_ref):
    for ch in range(8):
        cols = slice(ch * 256, (ch + 1) * 256)
        rows = jnp.stack([c_ref[b, :, ch].astype(F32) for b in range(2)], axis=1)
        conv = rows.reshape(256, 128).T
        mixed = (k_ref[:, cols].astype(F32) * v_ref[:, cols].astype(F32)).astype(BF)
        joined = conv + s_ref[:, cols] * mixed.astype(F32)
        o_ref[:, cols] = (q_ref[:, cols].astype(F32) * joined).astype(BF)


def conv_kernel(x_ref, f_ref, o_ref, xf, hf, xs, tt, acc):
    PAD=256
    ROWS=1024
    for b in range(2):
        xf[b, 0:PAD, :] = jnp.zeros((PAD,128),F32)
        xf[b, PAD:, :] = x_ref[b*128:(b+1)*128].astype(F32).reshape(ROWS,128)
    fv = f_ref[...].astype(F32).reshape(128,1024)
    for q in range(8): hf[q] = fv[:, q*128:(q+1)*128]
    row_i = lax.broadcasted_iota(jnp.int32,(128,128),0)
    col_i = lax.broadcasted_iota(jnp.int32,(128,128),1)
    keep = col_i >= row_i

    def skew(c, m_s, q):
        row = hf[q, pl.ds(m_s*8 + c, 1), :]
        return pltpu.roll(jnp.broadcast_to(row,(128,128)), 0, 1, stride=1, stride_axis=0)

    def channel(c, _):
        for e0 in range(16):
            for b in range(2):
                for h in range(2):
                    v = xf[b, pl.ds(PAD + (h - 2*e0)*8 + c, 64, stride=16), :]
                    xs[b*64:(b+1)*64, e0*256+h*128:e0*256+(h+1)*128] = v.astype(BF)
        def build(s, carry):
            prev, gprev = carry
            for q in range(0,8,2):
                r0 = skew(c, s, q)
                g0 = jnp.where(keep, r0, prev).astype(BF)
                r1 = skew(c, s, q+1)
                g1 = jnp.where(keep, r1, r0).astype(BF)
                base = pl.multiple_of(s*1024 + q*128, 256)
                tt[pl.ds(base,128), 0:128] = g0
                tt[pl.ds(base+128,128), 128:256] = g0
                tt[pl.ds(base,128), 128:256] = g1
                tt[pl.ds(base+128,128), 0:128] = gprev
                prev, gprev = r1, g1
            return prev, gprev
        lax.fori_loop(0,16,build,(jnp.zeros((128,128),F32),jnp.zeros((128,128),BF)))
        for e1 in range(4):
            n = 64-16*e1
            lhs = xs[...].reshape(2,64,4096)[:, :n, :].reshape(2*n,4096)
            p = jnp.dot(lhs, tt[e1*4096:(e1+1)*4096,:], preferred_element_type=F32).reshape(2,n,256)
            if e1==0: acc[...] = p
            else: acc[:,16*e1:,:] += p
        for b in range(2):
            for h in range(2):
                xf[b, pl.ds(PAD + h*8 + c, 64, stride=16), :] = acc[b, :, h*128:(h+1)*128]
        return 0
    lax.fori_loop(0,8,channel,0)
    for b in range(2):
        o_ref[b*128:(b+1)*128] = xf[b, PAD:, :].reshape(128,8,128).astype(BF)


def conv(x, f):
    return pl.pallas_call(
        conv_kernel,
        out_shape=jax.ShapeDtypeStruct((256, 8, 128), BF),
        in_specs=[VM, VM],
        out_specs=VM,
        scratch_shapes=[
            pltpu.VMEM((2, 1280, 128), F32),
            pltpu.VMEM((8, 128, 128), F32),
            pltpu.VMEM((128, 4096), BF),
            pltpu.VMEM((16384, 256), BF),
            pltpu.VMEM((2, 64, 256), F32),
        ],
        compiler_params=pltpu.CompilerParams(vmem_limit_bytes=40 * 2**20),
    )(x, f)


def body(query_gate, key_gate, value_input, long_filter, skip_gain):
    q, k, v = query_gate[0], key_gate[0], value_input[0]
    params = pltpu.CompilerParams(vmem_limit_bytes=40 * 2**20)
    own = lax.axis_index("batch").astype(jnp.int32).reshape(1)
    taps = pl.pallas_call(
        filter_kernel,
        out_shape=jax.ShapeDtypeStruct((16, 8, 1024), BF),
        in_specs=[pl.BlockSpec(memory_space=pltpu.SMEM), VM],
        out_specs=VM,
        compiler_params=params,
    )(own, long_filter)
    taps = lax.all_to_all(taps, "seq", split_axis=0, concat_axis=0, tiled=True)
    mixed = pl.pallas_call(
        mix_kernel,
        out_shape=jax.ShapeDtypeStruct((2, 16, 8, 8, 128), BF),
        in_specs=[VM, VM],
        out_specs=VM,
        compiler_params=params,
    )(k, v).reshape(256, 8, 128)
    mixed = lax.all_to_all(mixed, ALL, split_axis=0, concat_axis=0, tiled=True)
    conv_out = conv(mixed, taps)
    back = lax.all_to_all(conv_out, ALL, split_axis=0, concat_axis=0, tiled=True)
    return pl.pallas_call(
        gate_kernel,
        out_shape=jax.ShapeDtypeStruct((128, 2048), BF),
        in_specs=[VM] * 5,
        out_specs=VM,
        compiler_params=params,
    )(back.reshape(2, 16, 8, 8, 128), q, k, v, skip_gain.reshape(1, 2048))[None]


def solution(mesh):
    return jax.shard_map(
        body,
        mesh=mesh,
        in_specs=(
            P("batch", ("seq", "ch"), None),
            P("batch", ("seq", "ch"), None),
            P("batch", ("seq", "ch"), None),
            P("seq", "ch"),
            P(),
        ),
        out_specs=P("batch", ("seq", "ch"), None),
        check_vma=False,
    )
```

time: 490 us -> 120 us (0.24); the launches traced: 482 us -> 120 us
  waiting for transfers between devices: 261 us -> 9.24 us
  starting transfers between devices: 68.8 us -> 9.19 us
  local copies, waits for them, and re-layouts: 48.2 us -> 1.06 us
  matrix products: 45.2 us -> 0 us
  Pallas kernels: 0 us -> 43.2 us
  other arithmetic: 25.4 us -> 0 us
  blocking collectives: 32.6 us -> 57.3 us
    all_to_all x6 -> x1, waiting for transfers between devices: 261 us -> 9.24 us  [body(): taps = lax.all_to_all(taps, 'seq', split_axis=0, concat_axis=0, tiled=True)]
    all_to_all x6 -> x1, starting transfers between devices: 68.8 us -> 9.19 us  [body(): taps = lax.all_to_all(taps, 'seq', split_axis=0, concat_axis=0, tiled=True)]
    dot_general x6 -> x0, matrix products: 45.2 us -> none  [the longest x4 37.5 us: ccontract(): jnp.einsum(form, table, pair, precision=HIGHEST, preferred_element_type=j...]
    pallas_call x0 -> x4, Pallas kernels: none -> 43.2 us  [the longest x1 40.9 us: conv(): pl.pallas_call(conv_kernel, out_shape=jax.ShapeDtypeStruct((256, 8, 128),...]
    all_to_all x1 -> x2, blocking collectives: 32.6 us -> 57.3 us  [the longest x1 31.4 us: body(): mixed = lax.all_to_all(mixed, ALL, split_axis=0, concat_axis=0, tiled=True)]
    all_to_all x9 -> x0, local copies, waits for them, and re-layouts: 20 us -> none  [the longest x3 14.3 us: body(): lax.all_to_all(unrotated, 'seq', split_axis=2, concat_axis=1, tiled=True)]
    unnamed x3 -> x0, other arithmetic: 11.4 us -> none
    another operation x2 -> x0, local copies, waits for them, and re-layouts: 10.1 us -> none  [rotate(): jnp.stack([real_part * cos_tab + sense * imag_part * sin_tab, imag_part *...]
  transfers between devices with their start and end apart: 6 -> 1, of which waited for: 6 -> 1; matrix products, arithmetic and copies ran while one was open for 3% -> 0% of each run, Pallas kernels for 0% -> 0%
where the time goes in v1:
time: 120 us
  blocking collectives  57.3 us (48%)
  Pallas kernels  43.2 us (36%)
  waiting for transfers between devices  9.24 us (8%)
  starting transfers between devices  9.19 us (8%)
    pallas_call x1, Pallas kernels, conv(): pl.pallas_call(conv_kernel, out_shape=jax.ShapeDtypeStruct((256, 8, 128),...  40.9 us
    all_to_all x1, blocking collectives, body(): mixed = lax.all_to_all(mixed, ALL, split_axis=0, concat_axis=0, tiled=True)  31.4 us
    all_to_all x1, blocking collectives, body(): lax.all_to_all(conv_out, ALL, split_axis=0, concat_axis=0, tiled=True)  25.9 us
    all_to_all x1, waiting for transfers between devices, body(): taps = lax.all_to_all(taps, 'seq', split_axis=0, concat_axis=0, tiled=True)  9.24 us
    all_to_all x1, starting transfers between devices, body(): taps = lax.all_to_all(taps, 'seq', split_axis=0, concat_axis=0, tiled=True)  9.19 us
  transfers between devices with their start and end apart: 1, of which 1 were waited for; matrix products, arithmetic and copies ran while one was open for 0% of the time, Pallas kernels for 0%

profile of v1, /device:TPU:1, one launch (start us, length us, event | category | flops | bytes accessed | tf_op | source)
XLA Modules:
  0.0 120.1 jit_solution(4226198739668863020)
XLA Ops:
  0.0 0.0 copy-start.3
  0.0 1.0 copy-done.3
  1.0 0.0 copy-start
  1.0 0.0 copy-start.1
  1.0 0.9 shard_map.56
  2.0 9.2 %all-to-all-start.1 = ((bf16[16,8,1024]{2,1,0:T(8,128)(2,1)}), bf16[16,8,1024]{2,1,0:T(8,128)(2,1)S(1)}, u32[]{:S(2)}, u32[]{:S(2)}) async-start(bf16[16,8,1024]{2,1,0:T(8,128)(2,1)} %shard_map.56), calls=%async_computation.1 | async-start | bytes 524288 | tf_op jit(solution)/shard_map/all_to_all | solution.py:118
  11.1 0.0 copy-done
  11.2 0.0 copy-done.1
  11.2 0.2 shard_map.55
  11.4 9.2 %all-to-all-done.1.f_ref = bf16[16,8,1024]{2,1,0:T(8,128)(2,1)S(1)} async-done(((bf16[16,8,1024]{2,1,0:T(8,128)(2,1)}), bf16[16,8,1024]{2,1,0:T(8,128)(2,1)S(1)}, u32[]{:S(2)}, u32[]{:S(2)}) %all-to-all-start.1) | async-done | bytes 262176 | tf_op jit(solution)/shard_map/all_to_all | solution.py:118
  20.6 31.4 %all_to_all.15.x_ref = bf16[256,8,128]{2,1,0:T(8,128)(2,1)S(1)} all-to-all(bf16[256,8,128]{2,1,0:T(8,128)(2,1)S(1)} %bitcast.12), channel_id=1, replica_groups=mesh['seq'=16,'ch'=8,'batch'=2] {'batch','seq','ch'}, dimensions={0} | all-to-all | bytes 1048576 | tf_op jit(solution)/shard_map/all_to_all | solution.py:126
  52.0 40.9 %shard_map.57 = bf16[256,8,128]{2,1,0:T(8,128)(2,1)S(1)} custom-call(bf16[256,8,128]{2,1,0:T(8,128)(2,1)S(1)} %all_to_all.15.x_ref, bf16[16,8,1024]{2,1,0:T(8,128)(2,1)S(1)} %all-to-all-done.1.f_ref), custom_call_target="tpu_custom_call" | custom-call | tf_op jit(solution)/shard_map/pallas_call | solution.py:91
  93.0 0.0 copy-start.2
  93.0 0.0 copy-start.4
  93.0 25.9 %all_to_all.16 = bf16[256,8,128]{2,1,0:T(8,128)(2,1)S(1)} all-to-all(bf16[256,8,128]{2,1,0:T(8,128)(2,1)S(1)} %shard_map.57), channel_id=1, replica_groups=mesh['seq'=16,'ch'=8,'batch'=2] {'batch','seq','ch'}, dimensions={0} | all-to-all | bytes 1048576 | tf_op jit(solution)/shard_map/all_to_all | solution.py:128
  118.9 0.0 copy-done.2
  118.9 0.0 copy-done.4
  118.9 1.2 shard_map.58
Async XLA Ops:
  0.0 1.0 copy-start.3
  1.0 10.1 %copy-start = (bf16[1,128,2048]{2,1,0:T(8,128)(2,1)S(1)}, bf16[1,128,2048]{2,1,0:T(8,128)(2,1)}, u32[]{:S(2)}) copy-start(bf16[1,128,2048]{2,1,0:T(8,128)(2,1)} %param.6) | copy-start | bytes 1572868
  1.0 10.1 %copy-start.1 = (bf16[1,128,2048]{2,1,0:T(8,128)(2,1)S(1)}, bf16[1,128,2048]{2,1,0:T(8,128)(2,1)}, u32[]{:S(2)}) copy-start(bf16[1,128,2048]{2,1,0:T(8,128)(2,1)} %param.7) | copy-start | bytes 1572868
  2.0 18.7 %all-to-all-start.1 = ((bf16[16,8,1024]{2,1,0:T(8,128)(2,1)}), bf16[16,8,1024]{2,1,0:T(8,128)(2,1)S(1)}, u32[]{:S(2)}, u32[]{:S(2)}) async-start(bf16[16,8,1024]{2,1,0:T(8,128)(2,1)} %shard_map.56), calls=%async_computation.1 | async-start | bytes 524288 | tf_op jit(solution)/shard_map/all_to_all | solution.py:118
  93.0 26.0 %copy-start.2 = (bf16[1,128,2048]{2,1,0:T(8,128)(2,1)S(1)}, bf16[1,128,2048]{2,1,0:T(8,128)(2,1)}, u32[]{:S(2)}) copy-start(bf16[1,128,2048]{2,1,0:T(8,128)(2,1)} %param.5) | copy-start | bytes 1572868
  93.0 25.9 %copy-start.4 = (f32[2048]{0:T(1024)S(1)}, f32[2048]{0:T(1024)}, u32[]{:S(2)}) copy-start(f32[2048]{0:T(1024)} %param.9) | copy-start | bytes 24580

commit v2 on v1

--- a/solution.py
+++ b/solution.py
@@ -35,7 +35,7 @@
         o_ref[:, cols] = (q_ref[:, cols].astype(F32) * joined).astype(BF)
 
 
-def conv_kernel(x_ref, f_ref, o_ref, xf, hf, xs, tt, acc):
+def conv_kernel(x_ref, f_ref, o_ref, xf, hf, xa, xb, yf):
     PAD=256
     ROWS=1024
     for b in range(2):
@@ -47,44 +47,50 @@
     col_i = lax.broadcasted_iota(jnp.int32,(128,128),1)
     keep = col_i >= row_i
 
-    def skew(c, m_s, q):
-        row = hf[q, pl.ds(m_s*8 + c, 1), :]
+    def skew(c, m):
+        row = hf[m%8, pl.ds((m//8)*8 + c, 1), :]
         return pltpu.roll(jnp.broadcast_to(row,(128,128)), 0, 1, stride=1, stride_axis=0)
 
-    def channel(c, _):
-        for e0 in range(16):
-            for b in range(2):
-                for h in range(2):
-                    v = xf[b, pl.ds(PAD + (h - 2*e0)*8 + c, 64, stride=16), :]
-                    xs[b*64:(b+1)*64, e0*256+h*128:e0*256+(h+1)*128] = v.astype(BF)
-        def build(s, carry):
-            prev, gprev = carry
-            for q in range(0,8,2):
-                r0 = skew(c, s, q)
-                g0 = jnp.where(keep, r0, prev).astype(BF)
-                r1 = skew(c, s, q+1)
-                g1 = jnp.where(keep, r1, r0).astype(BF)
-                base = pl.multiple_of(s*1024 + q*128, 256)
-                tt[pl.ds(base,128), 0:128] = g0
-                tt[pl.ds(base+128,128), 128:256] = g0
-                tt[pl.ds(base,128), 128:256] = g1
-                tt[pl.ds(base+128,128), 0:128] = gprev
-                prev, gprev = r1, g1
-            return prev, gprev
-        lax.fori_loop(0,16,build,(jnp.zeros((128,128),F32),jnp.zeros((128,128),BF)))
+    def shifted(c, xs, e0):
+        for b in range(2):
+            for h in range(2):
+                v = xf[b, pl.ds(PAD + (h - 2*e0)*8 + c, 64, stride=16), :]
+                xs[b*64:(b+1)*64, e0*256+h*128:e0*256+(h+1)*128] = v.astype(BF)
+
+    def channel(c, xs, nxt):
+        prev = jnp.zeros((128,128),F32); gprev=jnp.zeros((128,128),BF)
+        total=None
         for e1 in range(4):
             n = 64-16*e1
             lhs = xs[...].reshape(2,64,4096)[:, :n, :].reshape(2*n,4096)
-            p = jnp.dot(lhs, tt[e1*4096:(e1+1)*4096,:], preferred_element_type=F32).reshape(2,n,256)
-            if e1==0: acc[...] = p
-            else: acc[:,16*e1:,:] += p
-        for b in range(2):
-            for h in range(2):
-                xf[b, pl.ds(PAD + h*8 + c, 64, stride=16), :] = acc[b, :, h*128:(h+1)*128]
+            p=None
+            for e0 in range(16):
+                e=16*e1+e0
+                r0=skew(c,2*e); g0=jnp.where(keep,r0,prev).astype(BF)
+                r1=skew(c,2*e+1); g1=jnp.where(keep,r1,r0).astype(BF)
+                rhs = jnp.concatenate([jnp.concatenate([g0,g1],axis=1), jnp.concatenate([gprev,g0],axis=1)],axis=0)
+                prev=r1; gprev=g1
+                pp = jnp.dot(lhs[:, e0*256:(e0+1)*256], rhs, preferred_element_type=F32)
+                p = pp if p is None else p+pp
+                if nxt is not None and e0%4==3:
+                    shifted(c+1, nxt, e//4)
+            p=p.reshape(2,n,256)
+            for b in range(2):
+                for h in range(2):
+                    at=pl.ds((32*e1*8 + h*8) + c, n, stride=16)
+                    val=p[b,:,h*128:(h+1)*128]
+                    if e1==0: yf[b, at, :] = val
+                    else: yf[b, at, :] = yf[b, at, :] + val
+    for e0 in range(16): shifted(0, xa, e0)
+    def pair(i, _):
+        channel(2*i, xa, xb)
+        channel(2*i+1, xb, xa)
         return 0
-    lax.fori_loop(0,8,channel,0)
+    lax.fori_loop(0,3,pair,0)
+    channel(6, xa, xb)
+    channel(7, xb, None)
     for b in range(2):
-        o_ref[b*128:(b+1)*128] = xf[b, PAD:, :].reshape(128,8,128).astype(BF)
+        o_ref[b*128:(b+1)*128] = yf[b].reshape(128,8,128).astype(BF)
 
 
 def conv(x, f):
@@ -97,8 +103,8 @@
             pltpu.VMEM((2, 1280, 128), F32),
             pltpu.VMEM((8, 128, 128), F32),
             pltpu.VMEM((128, 4096), BF),
-            pltpu.VMEM((16384, 256), BF),
-            pltpu.VMEM((2, 64, 256), F32),
+            pltpu.VMEM((128, 4096), BF),
+            pltpu.VMEM((2, 1024, 128), F32),
         ],
         compiler_params=pltpu.CompilerParams(vmem_limit_bytes=40 * 2**20),
     )(x, f)

time: 120 us -> 96.3 us (0.80)
  Pallas kernels: 43.2 us -> 19.2 us
    pallas_call x1, Pallas kernels: 40.9 us -> 16.9 us  [conv(): pl.pallas_call(conv_kernel, out_shape=jax.ShapeDtypeStruct((256, 8, 128),...]
where the time goes in v2:
time: 96.3 us; the launch traced here: 96 us
  blocking collectives  57.3 us (60%)
  Pallas kernels  19.2 us (20%)
  waiting for transfers between devices  9.24 us (10%)
  starting transfers between devices  9.19 us (10%)
  local copies, waits for them, and re-layouts  1.06 us (1%)
    all_to_all x1, blocking collectives, body(): mixed = lax.all_to_all(mixed, ALL, split_axis=0, concat_axis=0, tiled=True)  31.4 us
    all_to_all x1, blocking collectives, body(): lax.all_to_all(conv_out, ALL, split_axis=0, concat_axis=0, tiled=True)  25.9 us
    pallas_call x1, Pallas kernels, conv(): pl.pallas_call(conv_kernel, out_shape=jax.ShapeDtypeStruct((256, 8, 128),...  16.9 us
    all_to_all x1, waiting for transfers between devices, body(): taps = lax.all_to_all(taps, 'seq', split_axis=0, concat_axis=0, tiled=True)  9.24 us
    all_to_all x1, starting transfers between devices, body(): taps = lax.all_to_all(taps, 'seq', split_axis=0, concat_axis=0, tiled=True)  9.19 us
  transfers between devices with their start and end apart: 1, of which 1 were waited for; matrix products, arithmetic and copies ran while one was open for 0% of the time, Pallas kernels for 0%

profile of v2, /device:TPU:1, one launch (start us, length us, event | category | flops | bytes accessed | tf_op | source)
XLA Modules:
  0.0 96.0 jit_solution(3711474359050419770)
XLA Ops:
  0.0 0.0 copy-start.3
  0.0 1.0 %copy-done.3 = bf16[1024,256]{1,0:T(8,128)(2,1)S(1)} copy-done((bf16[1024,256]{1,0:T(8,128)(2,1)S(1)}, bf16[1024,256]{1,0:T(8,128)(2,1)}, u32[]{:S(2)}) %copy-start.3) | copy-done | bytes 524312
  1.0 0.0 copy-start
  1.0 0.0 copy-start.1
  1.0 0.9 shard_map.56
  2.0 9.2 %all-to-all-start.1 = ((bf16[16,8,1024]{2,1,0:T(8,128)(2,1)}), bf16[16,8,1024]{2,1,0:T(8,128)(2,1)S(1)}, u32[]{:S(2)}, u32[]{:S(2)}) async-start(bf16[16,8,1024]{2,1,0:T(8,128)(2,1)} %shard_map.56), calls=%async_computation.1 | async-start | bytes 524288 | tf_op jit(solution)/shard_map/all_to_all | solution.py:124
  11.1 0.0 copy-done
  11.2 0.0 copy-done.1
  11.2 0.2 shard_map.55
  11.4 9.2 %all-to-all-done.1.f_ref = bf16[16,8,1024]{2,1,0:T(8,128)(2,1)S(1)} async-done(((bf16[16,8,1024]{2,1,0:T(8,128)(2,1)}), bf16[16,8,1024]{2,1,0:T(8,128)(2,1)S(1)}, u32[]{:S(2)}, u32[]{:S(2)}) %all-to-all-start.1) | async-done | bytes 262176 | tf_op jit(solution)/shard_map/all_to_all | solution.py:124
  20.6 31.4 %all_to_all.15.x_ref = bf16[256,8,128]{2,1,0:T(8,128)(2,1)S(1)} all-to-all(bf16[256,8,128]{2,1,0:T(8,128)(2,1)S(1)} %bitcast.12), channel_id=1, replica_groups=mesh['seq'=16,'ch'=8,'batch'=2] {'batch','seq','ch'}, dimensions={0} | all-to-all | bytes 1048576 | tf_op jit(solution)/shard_map/all_to_all | solution.py:132
  52.0 16.9 %shard_map.57 = bf16[256,8,128]{2,1,0:T(8,128)(2,1)S(1)} custom-call(bf16[256,8,128]{2,1,0:T(8,128)(2,1)S(1)} %all_to_all.15.x_ref, bf16[16,8,1024]{2,1,0:T(8,128)(2,1)S(1)} %all-to-all-done.1.f_ref), custom_call_target="tpu_custom_call" | custom-call | tf_op jit(solution)/shard_map/pallas_call | solution.py:97
  68.9 0.0 copy-start.2
  68.9 0.0 copy-start.4
  68.9 25.9 %all_to_all.16 = bf16[256,8,128]{2,1,0:T(8,128)(2,1)S(1)} all-to-all(bf16[256,8,128]{2,1,0:T(8,128)(2,1)S(1)} %shard_map.57), channel_id=1, replica_groups=mesh['seq'=16,'ch'=8,'batch'=2] {'batch','seq','ch'}, dimensions={0} | all-to-all | bytes 1048576 | tf_op jit(solution)/shard_map/all_to_all | solution.py:134
  94.8 0.0 copy-done.2
  94.8 0.0 copy-done.4
  94.8 1.2 %shard_map.58 = bf16[128,2048]{1,0:T(8,128)(2,1)} custom-call(bf16[2,16,8,8,128]{4,3,2,1,0:T(8,128)(2,1)S(1)} %bitcast.13, bf16[128,2048]{1,0:T(8,128)(2,1)S(1)} %bitcast.14, bf16[128,2048]{1,0:T(8,128)(2,1)S(1)} %bitcast.9, bf16[128,2048]{1,0:T(8,128)(2,1)S(1)} %bitcast.11, f32[1,2048]{1,0:T(1,128)S(1)} %bitcast.15), custom_call_target="tpu_custom_call" | custom-call | tf_op jit(solution)/shard_map/pallas_call | solution.py:135
Async XLA Ops:
  0.0 1.0 %copy-start.3 = (bf16[1024,256]{1,0:T(8,128)(2,1)S(1)}, bf16[1024,256]{1,0:T(8,128)(2,1)}, u32[]{:S(2)}) copy-start(bf16[1024,256]{1,0:T(8,128)(2,1)} %f_ref.1) | copy-start | bytes 1572868
  1.0 10.1 %copy-start = (bf16[1,128,2048]{2,1,0:T(8,128)(2,1)S(1)}, bf16[1,128,2048]{2,1,0:T(8,128)(2,1)}, u32[]{:S(2)}) copy-start(bf16[1,128,2048]{2,1,0:T(8,128)(2,1)} %param.6) | copy-start | bytes 1572868
  1.0 10.1 %copy-start.1 = (bf16[1,128,2048]{2,1,0:T(8,128)(2,1)S(1)}, bf16[1,128,2048]{2,1,0:T(8,128)(2,1)}, u32[]{:S(2)}) copy-start(bf16[1,128,2048]{2,1,0:T(8,128)(2,1)} %param.7) | copy-start | bytes 1572868
  2.0 18.7 %all-to-all-start.1 = ((bf16[16,8,1024]{2,1,0:T(8,128)(2,1)}), bf16[16,8,1024]{2,1,0:T(8,128)(2,1)S(1)}, u32[]{:S(2)}, u32[]{:S(2)}) async-start(bf16[16,8,1024]{2,1,0:T(8,128)(2,1)} %shard_map.56), calls=%async_computation.1 | async-start | bytes 524288 | tf_op jit(solution)/shard_map/all_to_all | solution.py:124
  68.9 25.9 %copy-start.2 = (bf16[1,128,2048]{2,1,0:T(8,128)(2,1)S(1)}, bf16[1,128,2048]{2,1,0:T(8,128)(2,1)}, u32[]{:S(2)}) copy-start(bf16[1,128,2048]{2,1,0:T(8,128)(2,1)} %param.5) | copy-start | bytes 1572868
  68.9 25.9 %copy-start.4 = (f32[2048]{0:T(1024)S(1)}, f32[2048]{0:T(1024)}, u32[]{:S(2)}) copy-start(f32[2048]{0:T(1024)} %param.9) | copy-start | bytes 24580

commit v3 on v2

v3 whole, which is shorter than its diff:
```python
import jax
import jax.numpy as jnp
from jax import lax
from jax.experimental import pallas as pl
from jax.experimental.pallas import tpu as pltpu
from jax.sharding import PartitionSpec as P

F32 = jnp.float32
BF = jnp.bfloat16
ALL = ("batch", "seq", "ch")
VM = pl.BlockSpec(memory_space=pltpu.VMEM)
ANY = pl.BlockSpec(memory_space=pl.ANY)


def start_kernel(f_ref, k_ref, v_ref, o0, o1, o2, o3, m_ref, fb, kb, vb, mb, sems):
    loads = [
        pltpu.make_async_copy(src, dst, sems.at[i])
        for i, (src, dst) in enumerate(((k_ref, kb), (v_ref, vb), (f_ref, fb)))
    ]
    for load in loads:
        load.start()
    loads[0].wait()
    loads[1].wait()
    for ch in range(8):
        cols = slice(ch * 256, (ch + 1) * 256)
        mixed = (kb[:, cols].astype(F32) * vb[:, cols].astype(F32)).astype(BF)
        turned = mixed.astype(F32).T.reshape(16, 2, 8, 128).astype(BF)
        for b in range(2):
            mb[b, :, ch] = turned[:, b]
    store = pltpu.make_async_copy(mb, m_ref, sems.at[3])
    store.start()
    loads[2].wait()
    turned = fb[...].astype(F32).T.reshape(16, 2, 8, 1024)
    own = jnp.where(lax.axis_index("batch") == 0, turned[:, 0], turned[:, 1]).astype(BF).reshape(4, 4, 8, 1024)
    for z in range(4):

        @pl.when(lax.axis_index("seq") // 4 == z)
        def _():
            for q, o_ref in enumerate((o0, o1, o2, o3)):
                o_ref[...] = own[z ^ q]

    store.wait()


def turn_kernel(*refs):
    for r in range(4):
        for q in range(4):
            refs[4 + r][q] = refs[q][(lax.axis_index("seq") % 4) ^ r]


def gate_kernel(c_ref, q_ref, k_ref, v_ref, s_ref, o_ref):
    for ch in range(8):
        cols = slice(ch * 256, (ch + 1) * 256)
        rows = jnp.stack([c_ref[b, :, ch].astype(F32) for b in range(2)], axis=1)
        conv = rows.reshape(256, 128).T
        mixed = (k_ref[:, cols].astype(F32) * v_ref[:, cols].astype(F32)).astype(BF)
        joined = conv + s_ref[:, cols] * mixed.astype(F32)
        o_ref[:, cols] = (q_ref[:, cols].astype(F32) * joined).astype(BF)


def read_taps(hf, f_refs):
    seq = lax.axis_index("seq")
    for y, f_ref in enumerate(f_refs):
        for z in range(4):
            block = ((seq // 4) ^ z) * 4 + ((seq % 4) ^ y)
            rows = pl.ds(pl.multiple_of(block * 8, 8), 8)
            fv = f_ref[z].astype(F32)
            for q in range(8):
                hf[q, rows, :] = fv[:, q * 128 : (q + 1) * 128]


def upper():
    shape = (128, 128)
    return lax.broadcasted_iota(jnp.int32, shape, 1) >= lax.broadcasted_iota(jnp.int32, shape, 0)


def skew(hf, c, m):
    row = hf[m % 8, pl.ds((m // 8) * 8 + c, 1), :]
    turned = pltpu.roll(jnp.broadcast_to(row, (128, 128)), 0, 1, stride=1, stride_axis=0)
    return turned.astype(BF)


def conv_kernel(x_ref, f0_ref, f1_ref, f2_ref, f3_ref, o_ref, xf, hf, xa, xb, yf):
    pad = 256
    for b in range(2):
        xf[b, 0:pad, :] = jnp.zeros((pad, 128), F32)
        xf[b, pad:, :] = x_ref[b * 128 : (b + 1) * 128].astype(F32).reshape(1024, 128)
    read_taps(hf, (f0_ref, f1_ref, f2_ref, f3_ref))
    keep = upper()

    def shifted(c, xs, e0):
        for b in range(2):
            for h in range(2):
                v = xf[b, pl.ds(pad + (h - 2 * e0) * 8 + c, 64, stride=16), :]
                xs[b * 64 : (b + 1) * 64, e0 * 256 + h * 128 : e0 * 256 + (h + 1) * 128] = v.astype(BF)

    def channel(c, xs, after, nxt):
        prev = jnp.zeros((128, 128), BF)
        gprev = jnp.zeros((128, 128), BF)
        for e1 in range(4):
            n = 64 - 16 * e1
            lhs = xs[...].reshape(2, 64, 4096)[:, :n, :].reshape(2 * n, 4096)
            total = None
            for e0 in range(16):
                e = 16 * e1 + e0
                r0 = skew(hf, c, 2 * e)
                g0 = jnp.where(keep, r0, prev)
                r1 = skew(hf, c, 2 * e + 1)
                g1 = jnp.where(keep, r1, r0)
                top = jnp.concatenate([g0, g1], axis=1)
                low = jnp.concatenate([gprev, g0], axis=1)
                prev, gprev = r1, g1
                rhs = jnp.concatenate([top, low], axis=0)
                part = jnp.dot(lhs[:, e0 * 256 : (e0 + 1) * 256], rhs, preferred_element_type=F32)
                total = part if total is None else total + part
                if e0 % 4 == 3:
                    shifted(after, nxt, e // 4)
            total = total.reshape(2, n, 256)
            for b in range(2):
                for h in range(2):
                    at = pl.ds(32 * e1 * 8 + h * 8 + c, n, stride=16)
                    part = total[b, :, h * 128 : (h + 1) * 128]
                    yf[b, at, :] = part if e1 == 0 else yf[b, at, :] + part

    for e0 in range(16):
        shifted(0, xa, e0)

    def pair(i, _):
        channel(2 * i, xa, 2 * i + 1, xb)
        channel(2 * i + 1, xb, jnp.minimum(2 * i + 2, 7), xa)
        return 0

    lax.fori_loop(0, 4, pair, 0)
    for b in range(2):
        o_ref[b * 128 : (b + 1) * 128] = yf[b].reshape(128, 8, 128).astype(BF)


def conv(x, fs):
    return pl.pallas_call(
        conv_kernel,
        out_shape=jax.ShapeDtypeStruct((256, 8, 128), BF),
        in_specs=[VM] * 5,
        out_specs=VM,
        scratch_shapes=[
            pltpu.VMEM((2, 1280, 128), F32),
            pltpu.VMEM((8, 128, 128), F32),
            pltpu.VMEM((128, 4096), BF),
            pltpu.VMEM((128, 4096), BF),
            pltpu.VMEM((2, 1024, 128), F32),
        ],
        compiler_params=pltpu.CompilerParams(vmem_limit_bytes=32 * 2**20),
    )(x, *fs)


def swap(parts, step):
    return [parts[0]] + [
        lax.ppermute(parts[r], "seq", [(i, i ^ (r * step)) for i in range(16)])
        for r in range(1, 4)
    ]


def body(query_gate, key_gate, value_input, long_filter, skip_gain):
    q, k, v = query_gate[0], key_gate[0], value_input[0]
    params = pltpu.CompilerParams(vmem_limit_bytes=40 * 2**20)
    quarter = jax.ShapeDtypeStruct((4, 8, 1024), BF)
    *parts, mixed = pl.pallas_call(
        start_kernel,
        out_shape=[quarter] * 4 + [jax.ShapeDtypeStruct((2, 16, 8, 8, 128), BF)],
        in_specs=[ANY] * 3,
        out_specs=[VM] * 4 + [ANY],
        scratch_shapes=[
            pltpu.VMEM((1024, 256), BF),
            pltpu.VMEM((128, 2048), BF),
            pltpu.VMEM((128, 2048), BF),
            pltpu.VMEM((2, 16, 8, 8, 128), BF),
            pltpu.SemaphoreType.DMA((4,)),
        ],
        compiler_params=pltpu.CompilerParams(vmem_limit_bytes=60 * 2**20),
    )(long_filter, k, v)
    parts = swap(parts, 4)
    parts = pl.pallas_call(
        turn_kernel,
        out_shape=[quarter] * 4,
        in_specs=[VM] * 4,
        out_specs=[VM] * 4,
        compiler_params=params,
        cost_estimate=pl.CostEstimate(flops=2 * 10**10, bytes_accessed=0, transcendentals=0),
    )(*parts)
    parts = swap(parts, 1)
    mixed = lax.all_to_all(mixed.reshape(256, 8, 128), ALL, split_axis=0, concat_axis=0, tiled=True)
    conv_out = conv(mixed, parts)
    back = lax.all_to_all(conv_out, ALL, split_axis=0, concat_axis=0, tiled=True)
    return pl.pallas_call(
        gate_kernel,
        out_shape=jax.ShapeDtypeStruct((128, 2048), BF),
        in_specs=[VM] * 5,
        out_specs=VM,
        compiler_params=params,
    )(back.reshape(2, 16, 8, 8, 128), q, k, v, skip_gain.reshape(1, 2048))[None]


def solution(mesh):
    return jax.shard_map(
        body,
        mesh=mesh,
        in_specs=(
            P("batch", ("seq", "ch"), None),
            P("batch", ("seq", "ch"), None),
            P("batch", ("seq", "ch"), None),
            P("seq", "ch"),
            P(),
        ),
        out_specs=P("batch", ("seq", "ch"), None),
        check_vma=False,
    )
```

time: 96.3 us -> 86 us (0.89)
  blocking collectives: 57.3 us -> 25.9 us
  starting transfers between devices: 9.19 us -> 24.1 us
  waiting for transfers between devices: 9.24 us -> 15.8 us
  local copies, waits for them, and re-layouts: 1.06 us -> 0.02 us
    all_to_all x1 -> x0, blocking collectives: 31.4 us -> none  [body(): mixed = lax.all_to_all(mixed, ALL, split_axis=0, concat_axis=0, tiled=True)]
    ppermute x0 -> x6, starting transfers between devices: none -> 9.51 us  [swap(): lax.ppermute(parts[r], 'seq', [(i, i ^ r * step) for i in range(16)])]
    ppermute x0 -> x6, waiting for transfers between devices: none -> 7.57 us  [swap(): lax.ppermute(parts[r], 'seq', [(i, i ^ r * step) for i in range(16)])]
    all_to_all x1, starting transfers between devices: 9.19 us -> 14.6 us  [body(): lax.all_to_all(mixed.reshape(256, 8, 128), ALL, split_axis=0, concat_axis...]
    pallas_call x2, Pallas kernels: 1.14 us -> 3 us  [the longest x1 2.96 us: body(): pl.pallas_call(start_kernel, out_shape=[quarter] * 4 + [jax.ShapeDtypeStr...]
    pallas_call x1, Pallas kernels: 16.9 us -> 15.7 us  [conv(): pl.pallas_call(conv_kernel, out_shape=jax.ShapeDtypeStruct((256, 8, 128),...]
    unnamed x10, local copies, waits for them, and re-layouts: 1.06 us -> 0.02 us
    all_to_all x1, waiting for transfers between devices: 9.24 us -> 8.26 us  [body(): lax.all_to_all(mixed.reshape(256, 8, 128), ALL, split_axis=0, concat_axis...]
  transfers between devices with their start and end apart: 1 -> 7, of which waited for: 1 -> 3; matrix products, arithmetic and copies ran while one was open for 0% -> 0% of each run, Pallas kernels for 0% -> 0%
where the time goes in v3:
time: 86 us; the launch traced here: 85.8 us
  blocking collectives  25.9 us (30%)
  starting transfers between devices  24.1 us (28%)
  Pallas kernels  19.9 us (23%)
  waiting for transfers between devices  15.8 us (18%)
    all_to_all x1, blocking collectives, body(): lax.all_to_all(conv_out, ALL, split_axis=0, concat_axis=0, tiled=True)  25.9 us
    pallas_call x1, Pallas kernels, conv(): pl.pallas_call(conv_kernel, out_shape=jax.ShapeDtypeStruct((256, 8, 128),...  15.7 us
    all_to_all x1, starting transfers between devices, body(): lax.all_to_all(mixed.reshape(256, 8, 128), ALL, split_axis=0, concat_axis...  14.6 us
    ppermute x6, starting transfers between devices, swap(): lax.ppermute(parts[r], 'seq', [(i, i ^ r * step) for i in range(16)])  9.51 us
    all_to_all x1, waiting for transfers between devices, body(): lax.all_to_all(mixed.reshape(256, 8, 128), ALL, split_axis=0, concat_axis...  8.26 us
    ppermute x6, waiting for transfers between devices, swap(): lax.ppermute(parts[r], 'seq', [(i, i ^ r * step) for i in range(16)])  7.57 us
    pallas_call x1, Pallas kernels, body(): pl.pallas_call(start_kernel, out_shape=[quarter] * 4 + [jax.ShapeDtypeStr...  2.96 us
  transfers between devices with their start and end apart: 7, of which 3 were waited for; matrix products, arithmetic and copies ran while one was open for 0% of the time, Pallas kernels for 0%

profile of v3, /device:TPU:1, one launch (start us, length us, event | category | flops | bytes accessed | tf_op | source)
XLA Modules:
  0.0 85.8 jit_solution(5389048293179798335)
XLA Ops:
  0.0 3.0 %shard_map.55 = (bf16[4,8,1024]{2,1,0:T(8,128)(2,1)}, bf16[4,8,1024]{2,1,0:T(8,128)(2,1)}, bf16[4,8,1024]{2,1,0:T(8,128)(2,1)}, bf16[4,8,1024]{2,1,0:T(8,128)(2,1)}, bf16[2,16,8,8,128]{4,3,2,1,0:T(8,128)(2,1)}) custom-call(bf16[1024,256]{1,0:T(8,128)(2,1)} %f_ref.1, bf16[128,2048]{1,0:T(8,128)(2,1)} %bitcast.7, bf16[128,2048]{1,0:T(8,128)(2,1)} %bitcast.9), custom_call_target="tpu_custom_call" | custom-call | tf_op jit(solution)/shard_map/pallas_call | solution.py:166
  3.0 2.6 %collective-permute-start = (bf16[4,8,1024]{2,1,0:T(8,128)(2,1)}, bf16[4,8,1024]{2,1,0:T(8,128)(2,1)S(1)}, u32[]{:S(2)}, u32[]{:S(2)}) collective-permute-start(bf16[4,8,1024]{2,1,0:T(8,128)(2,1)} %get-tuple-element.16), channel_id=1, source_target_pairs={{0,64},{16,80},{32,96},{48,112},{64,0},{80,16},{96,32},{112,48},{1... | collective-permute-start | bytes 196616 | tf_op jit(solution)/shard_map/ppermute | solution.py:157
  5.5 3.0 %collective-permute-start.1 = (bf16[4,8,1024]{2,1,0:T(8,128)(2,1)}, bf16[4,8,1024]{2,1,0:T(8,128)(2,1)S(1)}, u32[]{:S(2)}, u32[]{:S(2)}) collective-permute-start(bf16[4,8,1024]{2,1,0:T(8,128)(2,1)} %get-tuple-element.17), channel_id=1, source_target_pairs={{0,128},{16,144},{32,160},{48,176},{64,192},{80,208},{96,224},{112... | collective-permute-start | bytes 196616 | tf_op jit(solution)/shard_map/ppermute | solution.py:157
  8.5 0.0 collective-permute-start.2
  8.5 14.6 %all-to-all-start = ((bf16[256,8,128]{2,1,0:T(8,128)(2,1)}), bf16[256,8,128]{2,1,0:T(8,128)(2,1)S(1)}, u32[]{:S(2)}, u32[]{:S(2)}) async-start(bf16[256,8,128]{2,1,0:T(8,128)(2,1)} %bitcast.14), calls=%async_computation | async-start | bytes 1048576 | tf_op jit(solution)/shard_map/all_to_all | solution.py:190
  23.1 0.0 collective-permute-done.refs_1_
  23.1 0.0 collective-permute-done.1.refs_2_
  23.1 0.0 collective-permute-done.2.refs_3_
  23.1 0.0 copy-done.4
  23.2 1.5 %collective-permute-start.3 = (bf16[4,8,1024]{2,1,0:T(8,128)(2,1)S(1)}, bf16[4,8,1024]{2,1,0:T(8,128)(2,1)S(1)}, u32[]{:S(2)}, u32[]{:S(2)}) collective-permute-start(bf16[4,8,1024]{2,1,0:T(8,128)(2,1)S(1)} %get-tuple-element.20), channel_id=1, source_target_pairs={{0,16},{16,0},{32,48},{48,32},{64,80},{80,64},{96,112},{112,96},{1... | collective-permute-start | bytes 196616 | tf_op jit(solution)/shard_map/ppermute | solution.py:157
  24.7 2.4 %collective-permute-start.4 = (bf16[4,8,1024]{2,1,0:T(8,128)(2,1)S(1)}, bf16[4,8,1024]{2,1,0:T(8,128)(2,1)S(1)}, u32[]{:S(2)}, u32[]{:S(2)}) collective-permute-start(bf16[4,8,1024]{2,1,0:T(8,128)(2,1)S(1)} %get-tuple-element.21), channel_id=1, source_target_pairs={{0,32},{16,48},{32,0},{48,16},{64,96},{80,112},{96,64},{112,80},{1... | collective-permute-start | bytes 196616 | tf_op jit(solution)/shard_map/ppermute | solution.py:157
  27.1 0.0 collective-permute-start.5
  27.2 0.0 collective-permute-done.3.f1_ref
  27.2 4.3 %collective-permute-done.4.f2_ref = bf16[4,8,1024]{2,1,0:T(8,128)(2,1)S(1)} collective-permute-done((bf16[4,8,1024]{2,1,0:T(8,128)(2,1)S(1)}, bf16[4,8,1024]{2,1,0:T(8,128)(2,1)S(1)}, u32[]{:S(2)}, u32[]{:S(2)}) %collective-permute-start.4) | collective-permute-done | bytes 65568 | tf_op jit(solution)/shard_map/ppermute | solution.py:157
  31.5 3.2 %collective-permute-done.5.f3_ref = bf16[4,8,1024]{2,1,0:T(8,128)(2,1)S(1)} collective-permute-done((bf16[4,8,1024]{2,1,0:T(8,128)(2,1)S(1)}, bf16[4,8,1024]{2,1,0:T(8,128)(2,1)S(1)}, u32[]{:S(2)}, u32[]{:S(2)}) %collective-permute-start.5) | collective-permute-done | bytes 65568 | tf_op jit(solution)/shard_map/ppermute | solution.py:157
  34.7 8.3 %all-to-all-done.x_ref = bf16[256,8,128]{2,1,0:T(8,128)(2,1)S(1)} async-done(((bf16[256,8,128]{2,1,0:T(8,128)(2,1)}), bf16[256,8,128]{2,1,0:T(8,128)(2,1)S(1)}, u32[]{:S(2)}, u32[]{:S(2)}) %all-to-all-start) | async-done | bytes 524320 | tf_op jit(solution)/shard_map/all_to_all | solution.py:190
  43.0 15.7 %shard_map.57 = bf16[256,8,128]{2,1,0:T(8,128)(2,1)S(1)} custom-call(bf16[256,8,128]{2,1,0:T(8,128)(2,1)S(1)} %all-to-all-done.x_ref, bf16[4,8,1024]{2,1,0:T(8,128)(2,1)S(1)} %get-tuple-element.19.f0_ref, bf16[4,8,1024]{2,1,0:T(8,128)(2,1)S(1)} %collective-permute-done.3.f1_ref, bf16[4,8,1024]{2,1,0:T(8,128)(2,1)S(1)} %collective-permute-done.4.f2_ref, ...), custom_call_target="tpu_custom_call" | custom-call | tf_op jit(solution)/shard_map/pallas_call | solution.py:139
  58.7 0.0 copy-start
  58.7 0.0 copy-start.1
  58.7 25.9 %all_to_all.10 = bf16[256,8,128]{2,1,0:T(8,128)(2,1)S(1)} all-to-all(bf16[256,8,128]{2,1,0:T(8,128)(2,1)S(1)} %shard_map.57), channel_id=1, replica_groups=mesh['seq'=16,'ch'=8,'batch'=2] {'batch','seq','ch'}, dimensions={0} | all-to-all | bytes 1048576 | tf_op jit(solution)/shard_map/all_to_all | solution.py:192
  84.6 0.0 copy-done.2
  84.7 0.0 copy-done.3
  84.7 0.0 copy-done.1
  84.7 1.2 %shard_map.58 = bf16[128,2048]{1,0:T(8,128)(2,1)} custom-call(bf16[2,16,8,8,128]{4,3,2,1,0:T(8,128)(2,1)S(1)} %bitcast.11, bf16[128,2048]{1,0:T(8,128)(2,1)S(1)} %bitcast.12, bf16[128,2048]{1,0:T(8,128)(2,1)S(1)} %bitcast.8, bf16[128,2048]{1,0:T(8,128)(2,1)S(1)} %bitcast.10, f32[1,2048]{1,0:T(1,128)S(1)} %bitcast.13), custom_call_target="tpu_custom_call" | custom-call | tf_op jit(solution)/shard_map/pallas_call | solution.py:193
  (5 shorter events, 0.0 us)
Async XLA Ops:
  3.0 20.1 %collective-permute-start = (bf16[4,8,1024]{2,1,0:T(8,128)(2,1)}, bf16[4,8,1024]{2,1,0:T(8,128)(2,1)S(1)}, u32[]{:S(2)}, u32[]{:S(2)}) collective-permute-start(bf16[4,8,1024]{2,1,0:T(8,128)(2,1)} %get-tuple-element.16), channel_id=1, source_target_pairs={{0,64},{16,80},{32,96},{48,112},{64,0},{80,16},{96,32},{112,48},{1... | collective-permute-start | bytes 196616 | tf_op jit(solution)/shard_map/ppermute | solution.py:157
  5.5 17.6 %collective-permute-start.1 = (bf16[4,8,1024]{2,1,0:T(8,128)(2,1)}, bf16[4,8,1024]{2,1,0:T(8,128)(2,1)S(1)}, u32[]{:S(2)}, u32[]{:S(2)}) collective-permute-start(bf16[4,8,1024]{2,1,0:T(8,128)(2,1)} %get-tuple-element.17), channel_id=1, source_target_pairs={{0,128},{16,144},{32,160},{48,176},{64,192},{80,208},{96,224},{112... | collective-permute-start | bytes 196616 | tf_op jit(solution)/shard_map/ppermute | solution.py:157
  8.5 14.6 %collective-permute-start.2 = (bf16[4,8,1024]{2,1,0:T(8,128)(2,1)}, bf16[4,8,1024]{2,1,0:T(8,128)(2,1)S(1)}, u32[]{:S(2)}, u32[]{:S(2)}) collective-permute-start(bf16[4,8,1024]{2,1,0:T(8,128)(2,1)} %get-tuple-element.18), channel_id=1, source_target_pairs={{0,192},{16,208},{32,224},{48,240},{64,128},{80,144},{96,160},{112... | collective-permute-start | bytes 196616 | tf_op jit(solution)/shard_map/ppermute | solution.py:157
  8.5 14.6 %copy-start.4 = (bf16[4,8,1024]{2,1,0:T(8,128)(2,1)S(1)}, bf16[4,8,1024]{2,1,0:T(8,128)(2,1)}, u32[]{:S(2)}) copy-start(bf16[4,8,1024]{2,1,0:T(8,128)(2,1)} %get-tuple-element.15.refs_0_) | copy-start | bytes 196612
  8.5 34.5 %all-to-all-start = ((bf16[256,8,128]{2,1,0:T(8,128)(2,1)}), bf16[256,8,128]{2,1,0:T(8,128)(2,1)S(1)}, u32[]{:S(2)}, u32[]{:S(2)}) async-start(bf16[256,8,128]{2,1,0:T(8,128)(2,1)} %bitcast.14), calls=%async_computation | async-start | bytes 1048576 | tf_op jit(solution)/shard_map/all_to_all | solution.py:190
  23.2 4.0 %collective-permute-start.3 = (bf16[4,8,1024]{2,1,0:T(8,128)(2,1)S(1)}, bf16[4,8,1024]{2,1,0:T(8,128)(2,1)S(1)}, u32[]{:S(2)}, u32[]{:S(2)}) collective-permute-start(bf16[4,8,1024]{2,1,0:T(8,128)(2,1)S(1)} %get-tuple-element.20), channel_id=1, source_target_pairs={{0,16},{16,0},{32,48},{48,32},{64,80},{80,64},{96,112},{112,96},{1... | collective-permute-start | bytes 196616 | tf_op jit(solution)/shard_map/ppermute | solution.py:157
  24.7 6.8 %collective-permute-start.4 = (bf16[4,8,1024]{2,1,0:T(8,128)(2,1)S(1)}, bf16[4,8,1024]{2,1,0:T(8,128)(2,1)S(1)}, u32[]{:S(2)}, u32[]{:S(2)}) collective-permute-start(bf16[4,8,1024]{2,1,0:T(8,128)(2,1)S(1)} %get-tuple-element.21), channel_id=1, source_target_pairs={{0,32},{16,48},{32,0},{48,16},{64,96},{80,112},{96,64},{112,80},{1... | collective-permute-start | bytes 196616 | tf_op jit(solution)/shard_map/ppermute | solution.py:157
  27.1 7.6 %collective-permute-start.5 = (bf16[4,8,1024]{2,1,0:T(8,128)(2,1)S(1)}, bf16[4,8,1024]{2,1,0:T(8,128)(2,1)S(1)}, u32[]{:S(2)}, u32[]{:S(2)}) collective-permute-start(bf16[4,8,1024]{2,1,0:T(8,128)(2,1)S(1)} %get-tuple-element.22), channel_id=1, source_target_pairs={{0,48},{16,32},{32,16},{48,0},{64,112},{80,96},{96,80},{112,64},{1... | collective-permute-start | bytes 196616 | tf_op jit(solution)/shard_map/ppermute | solution.py:157
  43.0 41.7 %copy-start.2 = (bf16[1,128,2048]{2,1,0:T(8,128)(2,1)S(1)}, bf16[1,128,2048]{2,1,0:T(8,128)(2,1)}, u32[]{:S(2)}) copy-start(bf16[1,128,2048]{2,1,0:T(8,128)(2,1)} %param.5) | copy-start | bytes 1572868
  43.0 41.7 %copy-start.3 = (f32[2048]{0:T(1024)S(1)}, f32[2048]{0:T(1024)}, u32[]{:S(2)}) copy-start(f32[2048]{0:T(1024)} %param.9) | copy-start | bytes 24580
  58.7 25.9 %copy-start = (bf16[1,128,2048]{2,1,0:T(8,128)(2,1)S(1)}, bf16[1,128,2048]{2,1,0:T(8,128)(2,1)}, u32[]{:S(2)}) copy-start(bf16[1,128,2048]{2,1,0:T(8,128)(2,1)} %param.6) | copy-start | bytes 1572868
  58.7 25.9 %copy-start.1 = (bf16[1,128,2048]{2,1,0:T(8,128)(2,1)S(1)}, bf16[1,128,2048]{2,1,0:T(8,128)(2,1)}, u32[]{:S(2)}) copy-start(bf16[1,128,2048]{2,1,0:T(8,128)(2,1)} %param.7) | copy-start | bytes 1572868

commit v4 on v3

--- a/solution.py
+++ b/solution.py
@@ -7,39 +7,44 @@
 
 F32 = jnp.float32
 BF = jnp.bfloat16
+HOPS = (0, 1, -1, 2)
 ALL = ("batch", "seq", "ch")
 VM = pl.BlockSpec(memory_space=pltpu.VMEM)
 ANY = pl.BlockSpec(memory_space=pl.ANY)
 
 
-def start_kernel(f_ref, k_ref, v_ref, o0, o1, o2, o3, m_ref, fb, kb, vb, mb, sems):
-    loads = [
-        pltpu.make_async_copy(src, dst, sems.at[i])
-        for i, (src, dst) in enumerate(((k_ref, kb), (v_ref, vb), (f_ref, fb)))
-    ]
+def start_kernel(f_ref, k_ref, v_ref, o0, o1, o2, o3, m_ref, fb, kb, vb, mb, ob, sems):
+    loads = []
+    for part in range(2):
+        cols = pl.ds(part * 1024, 1024)
+        for src, dst in ((k_ref, kb), (v_ref, vb)):
+            loads.append(pltpu.make_async_copy(src.at[:, cols], dst.at[:, cols], sems.at[len(loads)]))
+    loads.append(pltpu.make_async_copy(f_ref, fb, sems.at[4]))
     for load in loads:
         load.start()
-    loads[0].wait()
-    loads[1].wait()
-    for ch in range(8):
-        cols = slice(ch * 256, (ch + 1) * 256)
-        mixed = (kb[:, cols].astype(F32) * vb[:, cols].astype(F32)).astype(BF)
-        turned = mixed.astype(F32).T.reshape(16, 2, 8, 128).astype(BF)
-        for b in range(2):
-            mb[b, :, ch] = turned[:, b]
-    store = pltpu.make_async_copy(mb, m_ref, sems.at[3])
-    store.start()
-    loads[2].wait()
-    turned = fb[...].astype(F32).T.reshape(16, 2, 8, 1024)
-    own = jnp.where(lax.axis_index("batch") == 0, turned[:, 0], turned[:, 1]).astype(BF).reshape(4, 4, 8, 1024)
-    for z in range(4):
-
-        @pl.when(lax.axis_index("seq") // 4 == z)
-        def _():
-            for q, o_ref in enumerate((o0, o1, o2, o3)):
-                o_ref[...] = own[z ^ q]
-
-    store.wait()
+    stores = []
+    for part in range(2):
+        loads[2 * part].wait()
+        loads[2 * part + 1].wait()
+        for ch in range(4 * part, 4 * part + 4):
+            cols = slice(ch * 256, (ch + 1) * 256)
+            mixed = (kb[:, cols].astype(F32) * vb[:, cols].astype(F32)).astype(BF)
+            turned = mixed.astype(F32).T.reshape(16, 2, 8, 128).astype(BF)
+            for b in range(2):
+                mb[b, :, ch] = turned[:, b]
+        at = (slice(None), slice(None), pl.ds(4 * part, 4))
+        stores.append(pltpu.make_async_copy(mb.at[at], m_ref.at[at], sems.at[5 + part]))
+        stores[-1].start()
+    loads[4].wait()
+    turned = fb[...].astype(F32).T.reshape(16, 2, 8, 1024).astype(BF)
+    for b in range(2):
+        ob[b] = turned[:, b]
+    ring = lax.axis_index("batch") * 4 + lax.axis_index("seq") // 4
+    for o_ref, hop in zip((o0, o1, o2, o3), HOPS):
+        to = (ring + (hop + 8)) % 8
+        o_ref[...] = ob[to // 4, pl.ds((to % 4) * 4, 4)]
+    for store in stores:
+        store.wait()
 
 
 def turn_kernel(*refs):
@@ -61,8 +66,8 @@
 def read_taps(hf, f_refs):
     seq = lax.axis_index("seq")
     for y, f_ref in enumerate(f_refs):
-        for z in range(4):
-            block = ((seq // 4) ^ z) * 4 + ((seq % 4) ^ y)
+        for z, hop in enumerate(HOPS):
+            block = ((seq // 4 + (8 - hop)) % 4) * 4 + ((seq % 4) ^ y)
             rows = pl.ds(pl.multiple_of(block * 8, 8), 8)
             fv = f_ref[z].astype(F32)
             for q in range(8):
@@ -80,21 +85,26 @@
     return turned.astype(BF)
 
 
-def conv_kernel(x_ref, f0_ref, f1_ref, f2_ref, f3_ref, o_ref, xf, hf, xa, xb, yf):
-    pad = 256
+def conv_kernel(x_ref, f0_ref, f1_ref, f2_ref, f3_ref, o_ref, xf, hf, xa, xb, xg, yg, yf):
     for b in range(2):
-        xf[b, 0:pad, :] = jnp.zeros((pad, 128), F32)
-        xf[b, pad:, :] = x_ref[b * 128 : (b + 1) * 128].astype(F32).reshape(1024, 128)
+        xf[b] = x_ref[b * 128 : (b + 1) * 128].astype(F32).reshape(1024, 128)
+        for h in range(2):
+            xg[b, h, 0:16, :] = jnp.zeros((16, 128), F32)
     read_taps(hf, (f0_ref, f1_ref, f2_ref, f3_ref))
     keep = upper()
 
-    def shifted(c, xs, e0):
+    def pull(c):
         for b in range(2):
             for h in range(2):
-                v = xf[b, pl.ds(pad + (h - 2 * e0) * 8 + c, 64, stride=16), :]
-                xs[b * 64 : (b + 1) * 64, e0 * 256 + h * 128 : e0 * 256 + (h + 1) * 128] = v.astype(BF)
-
-    def channel(c, xs, after, nxt):
+                xg[b, h, 16:80, :] = xf[b, pl.ds(h * 8 + c, 64, stride=16), :]
+
+    def shifted(xs, e0):
+        for b in range(2):
+            for h in range(2):
+                cols = slice(e0 * 256 + h * 128, e0 * 256 + (h + 1) * 128)
+                xs[b * 64 : (b + 1) * 64, cols] = xg[b, h, 16 - e0 : 80 - e0, :].astype(BF)
+
+    def channel(c, xs, nxt):
         prev = jnp.zeros((128, 128), BF)
         gprev = jnp.zeros((128, 128), BF)
         for e1 in range(4):
@@ -113,24 +123,28 @@
                 rhs = jnp.concatenate([top, low], axis=0)
                 part = jnp.dot(lhs[:, e0 * 256 : (e0 + 1) * 256], rhs, preferred_element_type=F32)
                 total = part if total is None else total + part
-                if e0 % 4 == 3:
-                    shifted(after, nxt, e // 4)
+                if e == 1 and c < 7:
+                    pull(c + 1)
+                if e0 % 4 == 3 and c < 7:
+                    shifted(nxt, e // 4)
             total = total.reshape(2, n, 256)
             for b in range(2):
                 for h in range(2):
-                    at = pl.ds(32 * e1 * 8 + h * 8 + c, n, stride=16)
                     part = total[b, :, h * 128 : (h + 1) * 128]
-                    yf[b, at, :] = part if e1 == 0 else yf[b, at, :] + part
-
+                    if e1 == 0:
+                        yg[b, h] = part
+                    elif e1 < 3:
+                        yg[b, h, 16 * e1 :, :] += part
+                    else:
+                        yf[b, pl.ds(h * 8 + c, 48, stride=16), :] = yg[b, h, :48, :]
+                        yf[b, pl.ds(768 + h * 8 + c, 16, stride=16), :] = yg[b, h, 48:, :] + part
+
+    pull(0)
     for e0 in range(16):
-        shifted(0, xa, e0)
-
-    def pair(i, _):
-        channel(2 * i, xa, 2 * i + 1, xb)
-        channel(2 * i + 1, xb, jnp.minimum(2 * i + 2, 7), xa)
-        return 0
-
-    lax.fori_loop(0, 4, pair, 0)
+        shifted(xa, e0)
+
+    for c in range(8):
+        channel(c, (xa, xb)[c % 2], (xb, xa)[c % 2])
     for b in range(2):
         o_ref[b * 128 : (b + 1) * 128] = yf[b].reshape(128, 8, 128).astype(BF)
 
@@ -142,20 +156,31 @@
         in_specs=[VM] * 5,
         out_specs=VM,
         scratch_shapes=[
-            pltpu.VMEM((2, 1280, 128), F32),
+            pltpu.VMEM((2, 1024, 128), F32),
             pltpu.VMEM((8, 128, 128), F32),
             pltpu.VMEM((128, 4096), BF),
             pltpu.VMEM((128, 4096), BF),
+            pltpu.VMEM((2, 2, 80, 128), F32),
+            pltpu.VMEM((2, 2, 64, 128), F32),
             pltpu.VMEM((2, 1024, 128), F32),
         ],
         compiler_params=pltpu.CompilerParams(vmem_limit_bytes=32 * 2**20),
     )(x, *fs)
 
 
-def swap(parts, step):
+def along_z(parts):
+    def at(p, y):
+        return (p % 4 * 4 + y) * 2 + p % 8 // 4
+
     return [parts[0]] + [
-        lax.ppermute(parts[r], "seq", [(i, i ^ (r * step)) for i in range(16)])
-        for r in range(1, 4)
+        lax.ppermute(part, ("seq", "batch"), [(at(p, y), at(p + hop, y)) for p in range(8) for y in range(4)])
+        for part, hop in zip(parts[1:], HOPS[1:])
+    ]
+
+
+def along_y(parts):
+    return [parts[0]] + [
+        lax.ppermute(parts[r], "seq", [(i, i ^ r) for i in range(16)]) for r in range(1, 4)
     ]
 
 
@@ -173,11 +198,12 @@
             pltpu.VMEM((128, 2048), BF),
             pltpu.VMEM((128, 2048), BF),
             pltpu.VMEM((2, 16, 8, 8, 128), BF),
-            pltpu.SemaphoreType.DMA((4,)),
+            pltpu.VMEM((2, 16, 8, 1024), BF),
+            pltpu.SemaphoreType.DMA((7,)),
         ],
         compiler_params=pltpu.CompilerParams(vmem_limit_bytes=60 * 2**20),
     )(long_filter, k, v)
-    parts = swap(parts, 4)
+    parts = along_z(parts)
     parts = pl.pallas_call(
         turn_kernel,
         out_shape=[quarter] * 4,
@@ -186,7 +212,7 @@
         compiler_params=params,
         cost_estimate=pl.CostEstimate(flops=2 * 10**10, bytes_accessed=0, transcendentals=0),
     )(*parts)
-    parts = swap(parts, 1)
+    parts = along_y(parts)
     mixed = lax.all_to_all(mixed.reshape(256, 8, 128), ALL, split_axis=0, concat_axis=0, tiled=True)
     conv_out = conv(mixed, parts)
     back = lax.all_to_all(conv_out, ALL, split_axis=0, concat_axis=0, tiled=True)

time: 86 us -> 81.5 us (0.948)
  Pallas kernels: 19.9 us -> 16 us
    pallas_call x1, Pallas kernels: 15.7 us -> 12 us  [conv(): pl.pallas_call(conv_kernel, out_shape=jax.ShapeDtypeStruct((256, 8, 128),...]
    all_to_all x1, starting transfers between devices: 14.6 us -> 13 us  [body(): lax.all_to_all(mixed.reshape(256, 8, 128), ALL, split_axis=0, concat_axis...]
    ppermute x6, starting transfers between devices: 9.51 us -> 10.5 us  [the longest x3 6.57 us: along_z(): lax.ppermute(part, ('seq', 'batch'), [(at(p, y), at(p + hop, y)) for p in...]
where the time goes in v4:
time: 81.5 us; the launch traced here: 81.3 us
  blocking collectives  25.9 us (32%)
  starting transfers between devices  23.5 us (29%)
  Pallas kernels  16 us (20%)
  waiting for transfers between devices  15.8 us (19%)
    all_to_all x1, blocking collectives, body(): lax.all_to_all(conv_out, ALL, split_axis=0, concat_axis=0, tiled=True)  25.9 us
    all_to_all x1, starting transfers between devices, body(): lax.all_to_all(mixed.reshape(256, 8, 128), ALL, split_axis=0, concat_axis...  13 us
    pallas_call x1, Pallas kernels, conv(): pl.pallas_call(conv_kernel, out_shape=jax.ShapeDtypeStruct((256, 8, 128),...  12 us
    all_to_all x1, waiting for transfers between devices, body(): lax.all_to_all(mixed.reshape(256, 8, 128), ALL, split_axis=0, concat_axis...  8.26 us
    ppermute x3, waiting for transfers between devices, along_y(): lax.ppermute(parts[r], 'seq', [(i, i ^ r) for i in range(16)])  7.57 us
    ppermute x3, starting transfers between devices, along_z(): lax.ppermute(part, ('seq', 'batch'), [(at(p, y), at(p + hop, y)) for p in...  6.57 us
    ppermute x3, starting transfers between devices, along_y(): lax.ppermute(parts[r], 'seq', [(i, i ^ r) for i in range(16)])  3.97 us
    pallas_call x1, Pallas kernels, body(): pl.pallas_call(start_kernel, out_shape=[quarter] * 4 + [jax.ShapeDtypeStr...  2.79 us
  transfers between devices with their start and end apart: 7, of which 3 were waited for; matrix products, arithmetic and copies ran while one was open for 0% of the time, Pallas kernels for 0%

profile of v4, /device:TPU:1, one launch (start us, length us, event | category | flops | bytes accessed | tf_op | source)
XLA Modules:
  0.0 81.3 jit_solution(15652815749226757933)
XLA Ops:
  0.0 2.8 %shard_map.55 = (bf16[4,8,1024]{2,1,0:T(8,128)(2,1)}, bf16[4,8,1024]{2,1,0:T(8,128)(2,1)}, bf16[4,8,1024]{2,1,0:T(8,128)(2,1)}, bf16[4,8,1024]{2,1,0:T(8,128)(2,1)}, bf16[2,16,8,8,128]{4,3,2,1,0:T(8,128)(2,1)}) custom-call(bf16[1024,256]{1,0:T(8,128)(2,1)} %f_ref.1, bf16[128,2048]{1,0:T(8,128)(2,1)} %bitcast.7, bf16[128,2048]{1,0:T(8,128)(2,1)} %bitcast.9), custom_call_target="tpu_custom_call" | custom-call | tf_op jit(solution)/shard_map/pallas_call | solution.py:191
  2.8 2.5 %collective-permute-start = (bf16[4,8,1024]{2,1,0:T(8,128)(2,1)}, bf16[4,8,1024]{2,1,0:T(8,128)(2,1)S(1)}, u32[]{:S(2)}, u32[]{:S(2)}) collective-permute-start(bf16[4,8,1024]{2,1,0:T(8,128)(2,1)} %get-tuple-element.16), channel_id=1, source_target_pairs={{0,64},{16,80},{32,96},{48,112},{64,128},{80,144},{96,160},{112,17... | collective-permute-start | bytes 196616 | tf_op jit(solution)/shard_map/ppermute | solution.py:176
  5.3 4.0 %collective-permute-start.1 = (bf16[4,8,1024]{2,1,0:T(8,128)(2,1)}, bf16[4,8,1024]{2,1,0:T(8,128)(2,1)S(1)}, u32[]{:S(2)}, u32[]{:S(2)}) collective-permute-start(bf16[4,8,1024]{2,1,0:T(8,128)(2,1)} %get-tuple-element.17), channel_id=1, source_target_pairs={{0,193},{16,209},{32,225},{48,241},{64,0},{80,16},{96,32},{112,48}... | collective-permute-start | bytes 196616 | tf_op jit(solution)/shard_map/ppermute | solution.py:176
  9.4 0.0 collective-permute-start.2
  9.4 13.0 %all-to-all-start = ((bf16[256,8,128]{2,1,0:T(8,128)(2,1)}), bf16[256,8,128]{2,1,0:T(8,128)(2,1)S(1)}, u32[]{:S(2)}, u32[]{:S(2)}) async-start(bf16[256,8,128]{2,1,0:T(8,128)(2,1)} %bitcast.14), calls=%async_computation | async-start | bytes 1048576 | tf_op jit(solution)/shard_map/all_to_all | solution.py:216
  22.3 0.0 collective-permute-done.refs_1_
  22.4 0.0 collective-permute-done.1.refs_2_
  22.4 0.0 collective-permute-done.2.refs_3_
  22.4 0.0 copy-done.4
  22.4 1.5 %collective-permute-start.3 = (bf16[4,8,1024]{2,1,0:T(8,128)(2,1)S(1)}, bf16[4,8,1024]{2,1,0:T(8,128)(2,1)S(1)}, u32[]{:S(2)}, u32[]{:S(2)}) collective-permute-start(bf16[4,8,1024]{2,1,0:T(8,128)(2,1)S(1)} %get-tuple-element.20), channel_id=1, source_target_pairs={{0,16},{16,0},{32,48},{48,32},{64,80},{80,64},{96,112},{112,96},{1... | collective-permute-start | bytes 196616 | tf_op jit(solution)/shard_map/ppermute | solution.py:183
  23.9 2.4 %collective-permute-start.4 = (bf16[4,8,1024]{2,1,0:T(8,128)(2,1)S(1)}, bf16[4,8,1024]{2,1,0:T(8,128)(2,1)S(1)}, u32[]{:S(2)}, u32[]{:S(2)}) collective-permute-start(bf16[4,8,1024]{2,1,0:T(8,128)(2,1)S(1)} %get-tuple-element.21), channel_id=1, source_target_pairs={{0,32},{16,48},{32,0},{48,16},{64,96},{80,112},{96,64},{112,80},{1... | collective-permute-start | bytes 196616 | tf_op jit(solution)/shard_map/ppermute | solution.py:183
  26.4 0.0 collective-permute-start.5
  26.4 0.0 collective-permute-done.3.f1_ref
  26.4 4.3 %collective-permute-done.4.f2_ref = bf16[4,8,1024]{2,1,0:T(8,128)(2,1)S(1)} collective-permute-done((bf16[4,8,1024]{2,1,0:T(8,128)(2,1)S(1)}, bf16[4,8,1024]{2,1,0:T(8,128)(2,1)S(1)}, u32[]{:S(2)}, u32[]{:S(2)}) %collective-permute-start.4) | collective-permute-done | bytes 65568 | tf_op jit(solution)/shard_map/ppermute | solution.py:183
  30.7 3.2 %collective-permute-done.5.f3_ref = bf16[4,8,1024]{2,1,0:T(8,128)(2,1)S(1)} collective-permute-done((bf16[4,8,1024]{2,1,0:T(8,128)(2,1)S(1)}, bf16[4,8,1024]{2,1,0:T(8,128)(2,1)S(1)}, u32[]{:S(2)}, u32[]{:S(2)}) %collective-permute-start.5) | collective-permute-done | bytes 65568 | tf_op jit(solution)/shard_map/ppermute | solution.py:183
  34.0 8.3 %all-to-all-done.x_ref = bf16[256,8,128]{2,1,0:T(8,128)(2,1)S(1)} async-done(((bf16[256,8,128]{2,1,0:T(8,128)(2,1)}), bf16[256,8,128]{2,1,0:T(8,128)(2,1)S(1)}, u32[]{:S(2)}, u32[]{:S(2)}) %all-to-all-start) | async-done | bytes 524320 | tf_op jit(solution)/shard_map/all_to_all | solution.py:216
  42.2 12.0 %shard_map.57 = bf16[256,8,128]{2,1,0:T(8,128)(2,1)S(1)} custom-call(bf16[256,8,128]{2,1,0:T(8,128)(2,1)S(1)} %all-to-all-done.x_ref, bf16[4,8,1024]{2,1,0:T(8,128)(2,1)S(1)} %get-tuple-element.19.f0_ref, bf16[4,8,1024]{2,1,0:T(8,128)(2,1)S(1)} %collective-permute-done.3.f1_ref, bf16[4,8,1024]{2,1,0:T(8,128)(2,1)S(1)} %collective-permute-done.4.f2_ref, ...), custom_call_target="tpu_custom_call" | custom-call | tf_op jit(solution)/shard_map/pallas_call | solution.py:153
  54.2 0.0 copy-start
  54.2 0.0 copy-start.1
  54.2 25.9 %all_to_all.10 = bf16[256,8,128]{2,1,0:T(8,128)(2,1)S(1)} all-to-all(bf16[256,8,128]{2,1,0:T(8,128)(2,1)S(1)} %shard_map.57), channel_id=1, replica_groups=mesh['seq'=16,'ch'=8,'batch'=2] {'batch','seq','ch'}, dimensions={0} | all-to-all | bytes 1048576 | tf_op jit(solution)/shard_map/all_to_all | solution.py:218
  80.1 0.0 copy-done.2
  80.1 0.0 copy-done.3
  80.1 0.0 copy-done
  80.2 1.2 %shard_map.58 = bf16[128,2048]{1,0:T(8,128)(2,1)} custom-call(bf16[2,16,8,8,128]{4,3,2,1,0:T(8,128)(2,1)S(1)} %bitcast.11, bf16[128,2048]{1,0:T(8,128)(2,1)S(1)} %bitcast.12, bf16[128,2048]{1,0:T(8,128)(2,1)S(1)} %bitcast.8, bf16[128,2048]{1,0:T(8,128)(2,1)S(1)} %bitcast.10, f32[1,2048]{1,0:T(1,128)S(1)} %bitcast.13), custom_call_target="tpu_custom_call" | custom-call | tf_op jit(solution)/shard_map/pallas_call | solution.py:219
  (5 shorter events, 0.0 us)
Async XLA Ops:
  2.8 19.6 %collective-permute-start = (bf16[4,8,1024]{2,1,0:T(8,128)(2,1)}, bf16[4,8,1024]{2,1,0:T(8,128)(2,1)S(1)}, u32[]{:S(2)}, u32[]{:S(2)}) collective-permute-start(bf16[4,8,1024]{2,1,0:T(8,128)(2,1)} %get-tuple-element.16), channel_id=1, source_target_pairs={{0,64},{16,80},{32,96},{48,112},{64,128},{80,144},{96,160},{112,17... | collective-permute-start | bytes 196616 | tf_op jit(solution)/shard_map/ppermute | solution.py:176
  5.3 17.0 %collective-permute-start.1 = (bf16[4,8,1024]{2,1,0:T(8,128)(2,1)}, bf16[4,8,1024]{2,1,0:T(8,128)(2,1)S(1)}, u32[]{:S(2)}, u32[]{:S(2)}) collective-permute-start(bf16[4,8,1024]{2,1,0:T(8,128)(2,1)} %get-tuple-element.17), channel_id=1, source_target_pairs={{0,193},{16,209},{32,225},{48,241},{64,0},{80,16},{96,32},{112,48}... | collective-permute-start | bytes 196616 | tf_op jit(solution)/shard_map/ppermute | solution.py:176
  9.4 13.0 %collective-permute-start.2 = (bf16[4,8,1024]{2,1,0:T(8,128)(2,1)}, bf16[4,8,1024]{2,1,0:T(8,128)(2,1)S(1)}, u32[]{:S(2)}, u32[]{:S(2)}) collective-permute-start(bf16[4,8,1024]{2,1,0:T(8,128)(2,1)} %get-tuple-element.18), channel_id=1, source_target_pairs={{0,128},{16,144},{32,160},{48,176},{64,192},{80,208},{96,224},{112... | collective-permute-start | bytes 196616 | tf_op jit(solution)/shard_map/ppermute | solution.py:176
  9.4 13.0 %copy-start.4 = (bf16[4,8,1024]{2,1,0:T(8,128)(2,1)S(1)}, bf16[4,8,1024]{2,1,0:T(8,128)(2,1)}, u32[]{:S(2)}) copy-start(bf16[4,8,1024]{2,1,0:T(8,128)(2,1)} %get-tuple-element.15.refs_0_) | copy-start | bytes 196612
  9.4 32.9 %all-to-all-start = ((bf16[256,8,128]{2,1,0:T(8,128)(2,1)}), bf16[256,8,128]{2,1,0:T(8,128)(2,1)S(1)}, u32[]{:S(2)}, u32[]{:S(2)}) async-start(bf16[256,8,128]{2,1,0:T(8,128)(2,1)} %bitcast.14), calls=%async_computation | async-start | bytes 1048576 | tf_op jit(solution)/shard_map/all_to_all | solution.py:216
  22.4 4.0 %collective-permute-start.3 = (bf16[4,8,1024]{2,1,0:T(8,128)(2,1)S(1)}, bf16[4,8,1024]{2,1,0:T(8,128)(2,1)S(1)}, u32[]{:S(2)}, u32[]{:S(2)}) collective-permute-start(bf16[4,8,1024]{2,1,0:T(8,128)(2,1)S(1)} %get-tuple-element.20), channel_id=1, source_target_pairs={{0,16},{16,0},{32,48},{48,32},{64,80},{80,64},{96,112},{112,96},{1... | collective-permute-start | bytes 196616 | tf_op jit(solution)/shard_map/ppermute | solution.py:183
  23.9 6.8 %collective-permute-start.4 = (bf16[4,8,1024]{2,1,0:T(8,128)(2,1)S(1)}, bf16[4,8,1024]{2,1,0:T(8,128)(2,1)S(1)}, u32[]{:S(2)}, u32[]{:S(2)}) collective-permute-start(bf16[4,8,1024]{2,1,0:T(8,128)(2,1)S(1)} %get-tuple-element.21), channel_id=1, source_target_pairs={{0,32},{16,48},{32,0},{48,16},{64,96},{80,112},{96,64},{112,80},{1... | collective-permute-start | bytes 196616 | tf_op jit(solution)/shard_map/ppermute | solution.py:183
  26.4 7.6 %collective-permute-start.5 = (bf16[4,8,1024]{2,1,0:T(8,128)(2,1)S(1)}, bf16[4,8,1024]{2,1,0:T(8,128)(2,1)S(1)}, u32[]{:S(2)}, u32[]{:S(2)}) collective-permute-start(bf16[4,8,1024]{2,1,0:T(8,128)(2,1)S(1)} %get-tuple-element.22), channel_id=1, source_target_pairs={{0,48},{16,32},{32,16},{48,0},{64,112},{80,96},{96,80},{112,64},{1... | collective-permute-start | bytes 196616 | tf_op jit(solution)/shard_map/ppermute | solution.py:183
  42.2 37.9 %copy-start.2 = (bf16[1,128,2048]{2,1,0:T(8,128)(2,1)S(1)}, bf16[1,128,2048]{2,1,0:T(8,128)(2,1)}, u32[]{:S(2)}) copy-start(bf16[1,128,2048]{2,1,0:T(8,128)(2,1)} %param.5) | copy-start | bytes 1572868
  42.2 37.9 %copy-start.3 = (f32[2048]{0:T(1024)S(1)}, f32[2048]{0:T(1024)}, u32[]{:S(2)}) copy-start(f32[2048]{0:T(1024)} %param.9) | copy-start | bytes 24580
  54.2 25.9 %copy-start = (bf16[1,128,2048]{2,1,0:T(8,128)(2,1)S(1)}, bf16[1,128,2048]{2,1,0:T(8,128)(2,1)}, u32[]{:S(2)}) copy-start(bf16[1,128,2048]{2,1,0:T(8,128)(2,1)} %param.6) | copy-start | bytes 1572868
  54.2 25.9 %copy-start.1 = (bf16[1,128,2048]{2,1,0:T(8,128)(2,1)S(1)}, bf16[1,128,2048]{2,1,0:T(8,128)(2,1)}, u32[]{:S(2)}) copy-start(bf16[1,128,2048]{2,1,0:T(8,128)(2,1)} %param.7) | copy-start | bytes 1572868

commit v5 on v4

--- a/solution.py
+++ b/solution.py
@@ -7,25 +7,34 @@
 
 F32 = jnp.float32
 BF = jnp.bfloat16
-HOPS = (0, 1, -1, 2)
+HOPS = (0, 1, -1, -2)
 ALL = ("batch", "seq", "ch")
 VM = pl.BlockSpec(memory_space=pltpu.VMEM)
 ANY = pl.BlockSpec(memory_space=pl.ANY)
 
 
 def start_kernel(f_ref, k_ref, v_ref, o0, o1, o2, o3, m_ref, fb, kb, vb, mb, ob, sems):
-    loads = []
+    loads = [pltpu.make_async_copy(f_ref, fb, sems.at[0])]
     for part in range(2):
         cols = pl.ds(part * 1024, 1024)
         for src, dst in ((k_ref, kb), (v_ref, vb)):
             loads.append(pltpu.make_async_copy(src.at[:, cols], dst.at[:, cols], sems.at[len(loads)]))
-    loads.append(pltpu.make_async_copy(f_ref, fb, sems.at[4]))
     for load in loads:
         load.start()
+    loads[0].wait()
+    turned = fb[...].astype(F32).T.reshape(16, 2, 8, 1024).astype(BF)
+    for b in range(2):
+        ob[b] = turned[:, b]
+    ring = lax.axis_index("batch") * 4 + lax.axis_index("seq") // 4
     stores = []
+    for o_ref, hop in zip((o0, o1, o2, o3), HOPS):
+        to = (ring + (hop + 8)) % 8
+        src = ob.at[to // 4, pl.ds((to % 4) * 4, 4)]
+        stores.append(pltpu.make_async_copy(src, o_ref, sems.at[5 + len(stores)]))
+        stores[-1].start()
     for part in range(2):
-        loads[2 * part].wait()
         loads[2 * part + 1].wait()
+        loads[2 * part + 2].wait()
         for ch in range(4 * part, 4 * part + 4):
             cols = slice(ch * 256, (ch + 1) * 256)
             mixed = (kb[:, cols].astype(F32) * vb[:, cols].astype(F32)).astype(BF)
@@ -33,16 +42,8 @@
             for b in range(2):
                 mb[b, :, ch] = turned[:, b]
         at = (slice(None), slice(None), pl.ds(4 * part, 4))
-        stores.append(pltpu.make_async_copy(mb.at[at], m_ref.at[at], sems.at[5 + part]))
+        stores.append(pltpu.make_async_copy(mb.at[at], m_ref.at[at], sems.at[5 + len(stores)]))
         stores[-1].start()
-    loads[4].wait()
-    turned = fb[...].astype(F32).T.reshape(16, 2, 8, 1024).astype(BF)
-    for b in range(2):
-        ob[b] = turned[:, b]
-    ring = lax.axis_index("batch") * 4 + lax.axis_index("seq") // 4
-    for o_ref, hop in zip((o0, o1, o2, o3), HOPS):
-        to = (ring + (hop + 8)) % 8
-        o_ref[...] = ob[to // 4, pl.ds((to % 4) * 4, 4)]
     for store in stores:
         store.wait()
 
@@ -53,14 +54,21 @@
             refs[4 + r][q] = refs[q][(lax.axis_index("seq") % 4) ^ r]
 
 
-def gate_kernel(c_ref, q_ref, k_ref, v_ref, s_ref, o_ref):
+def gate_kernel(c_ref, q_ref, k_ref, v_ref, s_ref, o_ref, ob, sems):
+    stores = []
     for ch in range(8):
         cols = slice(ch * 256, (ch + 1) * 256)
         rows = jnp.stack([c_ref[b, :, ch].astype(F32) for b in range(2)], axis=1)
         conv = rows.reshape(256, 128).T
         mixed = (k_ref[:, cols].astype(F32) * v_ref[:, cols].astype(F32)).astype(BF)
         joined = conv + s_ref[:, cols] * mixed.astype(F32)
-        o_ref[:, cols] = (q_ref[:, cols].astype(F32) * joined).astype(BF)
+        ob[:, cols] = (q_ref[:, cols].astype(F32) * joined).astype(BF)
+        if ch % 2 == 1:
+            part = pl.ds((ch - 1) * 256, 512)
+            stores.append(pltpu.make_async_copy(ob.at[:, part], o_ref.at[:, part], sems.at[ch // 2]))
+            stores[-1].start()
+    for store in stores:
+        store.wait()
 
 
 def read_taps(hf, f_refs):
@@ -192,14 +200,14 @@
         start_kernel,
         out_shape=[quarter] * 4 + [jax.ShapeDtypeStruct((2, 16, 8, 8, 128), BF)],
         in_specs=[ANY] * 3,
-        out_specs=[VM] * 4 + [ANY],
+        out_specs=[ANY] * 5,
         scratch_shapes=[
             pltpu.VMEM((1024, 256), BF),
             pltpu.VMEM((128, 2048), BF),
             pltpu.VMEM((128, 2048), BF),
             pltpu.VMEM((2, 16, 8, 8, 128), BF),
             pltpu.VMEM((2, 16, 8, 1024), BF),
-            pltpu.SemaphoreType.DMA((7,)),
+            pltpu.SemaphoreType.DMA((11,)),
         ],
         compiler_params=pltpu.CompilerParams(vmem_limit_bytes=60 * 2**20),
     )(long_filter, k, v)
@@ -220,7 +228,8 @@
         gate_kernel,
         out_shape=jax.ShapeDtypeStruct((128, 2048), BF),
         in_specs=[VM] * 5,
-        out_specs=VM,
+        out_specs=ANY,
+        scratch_shapes=[pltpu.VMEM((128, 2048), BF), pltpu.SemaphoreType.DMA((4,))],
         compiler_params=params,
     )(back.reshape(2, 16, 8, 8, 128), q, k, v, skip_gain.reshape(1, 2048))[None]
 

time: 81.5 us -> 81.1 us (level)
    all_to_all x1, starting transfers between devices: 13 us -> 11.1 us  [body(): lax.all_to_all(mixed.reshape(256, 8, 128), ALL, split_axis=0, concat_axis...]
    ppermute x3, starting transfers between devices: 6.57 us -> 8.39 us  [along_z(): lax.ppermute(part, ('seq', 'batch'), [(at(p, y), at(p + hop, y)) for p in...]
where the time goes in v5:
time: 81.1 us; the launch traced here: 80.9 us
  blocking collectives  25.9 us (32%)
  starting transfers between devices  23.5 us (29%)
  waiting for transfers between devices  15.8 us (19%)
  Pallas kernels  15.4 us (19%)
    all_to_all x1, blocking collectives, body(): lax.all_to_all(conv_out, ALL, split_axis=0, concat_axis=0, tiled=True)  25.9 us
    pallas_call x1, Pallas kernels, conv(): pl.pallas_call(conv_kernel, out_shape=jax.ShapeDtypeStruct((256, 8, 128),...  12 us
    all_to_all x1, starting transfers between devices, body(): lax.all_to_all(mixed.reshape(256, 8, 128), ALL, split_axis=0, concat_axis...  11.1 us
    ppermute x3, starting transfers between devices, along_z(): lax.ppermute(part, ('seq', 'batch'), [(at(p, y), at(p + hop, y)) for p in...  8.39 us
    all_to_all x1, waiting for transfers between devices, body(): lax.all_to_all(mixed.reshape(256, 8, 128), ALL, split_axis=0, concat_axis...  8.26 us
    ppermute x3, waiting for transfers between devices, along_y(): lax.ppermute(parts[r], 'seq', [(i, i ^ r) for i in range(16)])  7.57 us
    ppermute x3, starting transfers between devices, along_y(): lax.ppermute(parts[r], 'seq', [(i, i ^ r) for i in range(16)])  3.97 us
    pallas_call x1, Pallas kernels, body(): pl.pallas_call(start_kernel, out_shape=[quarter] * 4 + [jax.ShapeDtypeStr...  2.33 us
  transfers between devices with their start and end apart: 7, of which 3 were waited for; matrix products, arithmetic and copies ran while one was open for 0% of the time, Pallas kernels for 0%

profile of v5, /device:TPU:1, one launch (start us, length us, event | category | flops | bytes accessed | tf_op | source)
XLA Modules:
  0.0 80.9 jit_solution(8945902233161635739)
XLA Ops:
  0.0 2.3 %shard_map.55 = (bf16[4,8,1024]{2,1,0:T(8,128)(2,1)}, bf16[4,8,1024]{2,1,0:T(8,128)(2,1)}, bf16[4,8,1024]{2,1,0:T(8,128)(2,1)}, bf16[4,8,1024]{2,1,0:T(8,128)(2,1)}, bf16[2,16,8,8,128]{4,3,2,1,0:T(8,128)(2,1)}) custom-call(bf16[1024,256]{1,0:T(8,128)(2,1)} %f_ref.1, bf16[128,2048]{1,0:T(8,128)(2,1)} %bitcast.7, bf16[128,2048]{1,0:T(8,128)(2,1)} %bitcast.9), custom_call_target="tpu_custom_call" | custom-call | tf_op jit(solution)/shard_map/pallas_call | solution.py:199
  2.3 2.5 %collective-permute-start = (bf16[4,8,1024]{2,1,0:T(8,128)(2,1)}, bf16[4,8,1024]{2,1,0:T(8,128)(2,1)S(1)}, u32[]{:S(2)}, u32[]{:S(2)}) collective-permute-start(bf16[4,8,1024]{2,1,0:T(8,128)(2,1)} %get-tuple-element.16), channel_id=1, source_target_pairs={{0,64},{16,80},{32,96},{48,112},{64,128},{80,144},{96,160},{112,17... | collective-permute-start | bytes 196616 | tf_op jit(solution)/shard_map/ppermute | solution.py:184
  4.9 4.0 %collective-permute-start.1 = (bf16[4,8,1024]{2,1,0:T(8,128)(2,1)}, bf16[4,8,1024]{2,1,0:T(8,128)(2,1)S(1)}, u32[]{:S(2)}, u32[]{:S(2)}) collective-permute-start(bf16[4,8,1024]{2,1,0:T(8,128)(2,1)} %get-tuple-element.17), channel_id=1, source_target_pairs={{0,193},{16,209},{32,225},{48,241},{64,0},{80,16},{96,32},{112,48}... | collective-permute-start | bytes 196616 | tf_op jit(solution)/shard_map/ppermute | solution.py:184
  8.9 1.8 %collective-permute-start.2 = (bf16[4,8,1024]{2,1,0:T(8,128)(2,1)}, bf16[4,8,1024]{2,1,0:T(8,128)(2,1)S(1)}, u32[]{:S(2)}, u32[]{:S(2)}) collective-permute-start(bf16[4,8,1024]{2,1,0:T(8,128)(2,1)} %get-tuple-element.18), channel_id=1, source_target_pairs={{0,129},{16,145},{32,161},{48,177},{64,193},{80,209},{96,225},{112... | collective-permute-start | bytes 196616 | tf_op jit(solution)/shard_map/ppermute | solution.py:184
  10.7 11.1 %all-to-all-start = ((bf16[256,8,128]{2,1,0:T(8,128)(2,1)}), bf16[256,8,128]{2,1,0:T(8,128)(2,1)S(1)}, u32[]{:S(2)}, u32[]{:S(2)}) async-start(bf16[256,8,128]{2,1,0:T(8,128)(2,1)} %bitcast.14), calls=%async_computation | async-start | bytes 1048576 | tf_op jit(solution)/shard_map/all_to_all | solution.py:224
  21.9 0.0 collective-permute-done.refs_1_
  21.9 0.0 collective-permute-done.1.refs_2_
  21.9 0.0 collective-permute-done.2.refs_3_
  21.9 0.0 copy-done.4
  22.0 1.5 %collective-permute-start.3 = (bf16[4,8,1024]{2,1,0:T(8,128)(2,1)S(1)}, bf16[4,8,1024]{2,1,0:T(8,128)(2,1)S(1)}, u32[]{:S(2)}, u32[]{:S(2)}) collective-permute-start(bf16[4,8,1024]{2,1,0:T(8,128)(2,1)S(1)} %get-tuple-element.20), channel_id=1, source_target_pairs={{0,16},{16,0},{32,48},{48,32},{64,80},{80,64},{96,112},{112,96},{1... | collective-permute-start | bytes 196616 | tf_op jit(solution)/shard_map/ppermute | solution.py:191
  23.4 2.4 %collective-permute-start.4 = (bf16[4,8,1024]{2,1,0:T(8,128)(2,1)S(1)}, bf16[4,8,1024]{2,1,0:T(8,128)(2,1)S(1)}, u32[]{:S(2)}, u32[]{:S(2)}) collective-permute-start(bf16[4,8,1024]{2,1,0:T(8,128)(2,1)S(1)} %get-tuple-element.21), channel_id=1, source_target_pairs={{0,32},{16,48},{32,0},{48,16},{64,96},{80,112},{96,64},{112,80},{1... | collective-permute-start | bytes 196616 | tf_op jit(solution)/shard_map/ppermute | solution.py:191
  25.9 0.0 collective-permute-start.5
  25.9 0.0 collective-permute-done.3.f1_ref
  25.9 4.3 %collective-permute-done.4.f2_ref = bf16[4,8,1024]{2,1,0:T(8,128)(2,1)S(1)} collective-permute-done((bf16[4,8,1024]{2,1,0:T(8,128)(2,1)S(1)}, bf16[4,8,1024]{2,1,0:T(8,128)(2,1)S(1)}, u32[]{:S(2)}, u32[]{:S(2)}) %collective-permute-start.4) | collective-permute-done | bytes 65568 | tf_op jit(solution)/shard_map/ppermute | solution.py:191
  30.3 3.2 %collective-permute-done.5.f3_ref = bf16[4,8,1024]{2,1,0:T(8,128)(2,1)S(1)} collective-permute-done((bf16[4,8,1024]{2,1,0:T(8,128)(2,1)S(1)}, bf16[4,8,1024]{2,1,0:T(8,128)(2,1)S(1)}, u32[]{:S(2)}, u32[]{:S(2)}) %collective-permute-start.5) | collective-permute-done | bytes 65568 | tf_op jit(solution)/shard_map/ppermute | solution.py:191
  33.5 8.3 %all-to-all-done.x_ref = bf16[256,8,128]{2,1,0:T(8,128)(2,1)S(1)} async-done(((bf16[256,8,128]{2,1,0:T(8,128)(2,1)}), bf16[256,8,128]{2,1,0:T(8,128)(2,1)S(1)}, u32[]{:S(2)}, u32[]{:S(2)}) %all-to-all-start) | async-done | bytes 524320 | tf_op jit(solution)/shard_map/all_to_all | solution.py:224
  41.8 12.0 %shard_map.57 = bf16[256,8,128]{2,1,0:T(8,128)(2,1)S(1)} custom-call(bf16[256,8,128]{2,1,0:T(8,128)(2,1)S(1)} %all-to-all-done.x_ref, bf16[4,8,1024]{2,1,0:T(8,128)(2,1)S(1)} %get-tuple-element.19.f0_ref, bf16[4,8,1024]{2,1,0:T(8,128)(2,1)S(1)} %collective-permute-done.3.f1_ref, bf16[4,8,1024]{2,1,0:T(8,128)(2,1)S(1)} %collective-permute-done.4.f2_ref, ...), custom_call_target="tpu_custom_call" | custom-call | tf_op jit(solution)/shard_map/pallas_call | solution.py:161
  53.8 0.0 copy-start
  53.8 0.0 copy-start.1
  53.8 25.9 %all_to_all.10 = bf16[256,8,128]{2,1,0:T(8,128)(2,1)S(1)} all-to-all(bf16[256,8,128]{2,1,0:T(8,128)(2,1)S(1)} %shard_map.57), channel_id=1, replica_groups=mesh['seq'=16,'ch'=8,'batch'=2] {'batch','seq','ch'}, dimensions={0} | all-to-all | bytes 1048576 | tf_op jit(solution)/shard_map/all_to_all | solution.py:226
  79.7 0.0 copy-done.2
  79.7 0.0 copy-done.3
  79.7 0.0 copy-done
  79.7 1.1 %shard_map.58 = bf16[128,2048]{1,0:T(8,128)(2,1)} custom-call(bf16[2,16,8,8,128]{4,3,2,1,0:T(8,128)(2,1)S(1)} %bitcast.11, bf16[128,2048]{1,0:T(8,128)(2,1)S(1)} %bitcast.12, bf16[128,2048]{1,0:T(8,128)(2,1)S(1)} %bitcast.8, bf16[128,2048]{1,0:T(8,128)(2,1)S(1)} %bitcast.10, f32[1,2048]{1,0:T(1,128)S(1)} %bitcast.13), custom_call_target="tpu_custom_call" | custom-call | tf_op jit(solution)/shard_map/pallas_call | solution.py:227
  (5 shorter events, 0.0 us)
Async XLA Ops:
  2.3 19.5 %collective-permute-start = (bf16[4,8,1024]{2,1,0:T(8,128)(2,1)}, bf16[4,8,1024]{2,1,0:T(8,128)(2,1)S(1)}, u32[]{:S(2)}, u32[]{:S(2)}) collective-permute-start(bf16[4,8,1024]{2,1,0:T(8,128)(2,1)} %get-tuple-element.16), channel_id=1, source_target_pairs={{0,64},{16,80},{32,96},{48,112},{64,128},{80,144},{96,160},{112,17... | collective-permute-start | bytes 196616 | tf_op jit(solution)/shard_map/ppermute | solution.py:184
  4.9 17.0 %collective-permute-start.1 = (bf16[4,8,1024]{2,1,0:T(8,128)(2,1)}, bf16[4,8,1024]{2,1,0:T(8,128)(2,1)S(1)}, u32[]{:S(2)}, u32[]{:S(2)}) collective-permute-start(bf16[4,8,1024]{2,1,0:T(8,128)(2,1)} %get-tuple-element.17), channel_id=1, source_target_pairs={{0,193},{16,209},{32,225},{48,241},{64,0},{80,16},{96,32},{112,48}... | collective-permute-start | bytes 196616 | tf_op jit(solution)/shard_map/ppermute | solution.py:184
  8.9 13.0 %collective-permute-start.2 = (bf16[4,8,1024]{2,1,0:T(8,128)(2,1)}, bf16[4,8,1024]{2,1,0:T(8,128)(2,1)S(1)}, u32[]{:S(2)}, u32[]{:S(2)}) collective-permute-start(bf16[4,8,1024]{2,1,0:T(8,128)(2,1)} %get-tuple-element.18), channel_id=1, source_target_pairs={{0,129},{16,145},{32,161},{48,177},{64,193},{80,209},{96,225},{112... | collective-permute-start | bytes 196616 | tf_op jit(solution)/shard_map/ppermute | solution.py:184
  10.7 11.2 %copy-start.4 = (bf16[4,8,1024]{2,1,0:T(8,128)(2,1)S(1)}, bf16[4,8,1024]{2,1,0:T(8,128)(2,1)}, u32[]{:S(2)}) copy-start(bf16[4,8,1024]{2,1,0:T(8,128)(2,1)} %get-tuple-element.15.refs_0_) | copy-start | bytes 196612
  10.7 31.0 %all-to-all-start = ((bf16[256,8,128]{2,1,0:T(8,128)(2,1)}), bf16[256,8,128]{2,1,0:T(8,128)(2,1)S(1)}, u32[]{:S(2)}, u32[]{:S(2)}) async-start(bf16[256,8,128]{2,1,0:T(8,128)(2,1)} %bitcast.14), calls=%async_computation | async-start | bytes 1048576 | tf_op jit(solution)/shard_map/all_to_all | solution.py:224
  22.0 4.0 %collective-permute-start.3 = (bf16[4,8,1024]{2,1,0:T(8,128)(2,1)S(1)}, bf16[4,8,1024]{2,1,0:T(8,128)(2,1)S(1)}, u32[]{:S(2)}, u32[]{:S(2)}) collective-permute-start(bf16[4,8,1024]{2,1,0:T(8,128)(2,1)S(1)} %get-tuple-element.20), channel_id=1, source_target_pairs={{0,16},{16,0},{32,48},{48,32},{64,80},{80,64},{96,112},{112,96},{1... | collective-permute-start | bytes 196616 | tf_op jit(solution)/shard_map/ppermute | solution.py:191
  23.4 6.8 %collective-permute-start.4 = (bf16[4,8,1024]{2,1,0:T(8,128)(2,1)S(1)}, bf16[4,8,1024]{2,1,0:T(8,128)(2,1)S(1)}, u32[]{:S(2)}, u32[]{:S(2)}) collective-permute-start(bf16[4,8,1024]{2,1,0:T(8,128)(2,1)S(1)} %get-tuple-element.21), channel_id=1, source_target_pairs={{0,32},{16,48},{32,0},{48,16},{64,96},{80,112},{96,64},{112,80},{1... | collective-permute-start | bytes 196616 | tf_op jit(solution)/shard_map/ppermute | solution.py:191
  25.9 7.6 %collective-permute-start.5 = (bf16[4,8,1024]{2,1,0:T(8,128)(2,1)S(1)}, bf16[4,8,1024]{2,1,0:T(8,128)(2,1)S(1)}, u32[]{:S(2)}, u32[]{:S(2)}) collective-permute-start(bf16[4,8,1024]{2,1,0:T(8,128)(2,1)S(1)} %get-tuple-element.22), channel_id=1, source_target_pairs={{0,48},{16,32},{32,16},{48,0},{64,112},{80,96},{96,80},{112,64},{1... | collective-permute-start | bytes 196616 | tf_op jit(solution)/shard_map/ppermute | solution.py:191
  41.8 37.9 %copy-start.2 = (bf16[1,128,2048]{2,1,0:T(8,128)(2,1)S(1)}, bf16[1,128,2048]{2,1,0:T(8,128)(2,1)}, u32[]{:S(2)}) copy-start(bf16[1,128,2048]{2,1,0:T(8,128)(2,1)} %param.5) | copy-start | bytes 1572868
  41.8 37.9 %copy-start.3 = (f32[2048]{0:T(1024)S(1)}, f32[2048]{0:T(1024)}, u32[]{:S(2)}) copy-start(f32[2048]{0:T(1024)} %param.9) | copy-start | bytes 24580
  53.8 25.9 %copy-start = (bf16[1,128,2048]{2,1,0:T(8,128)(2,1)S(1)}, bf16[1,128,2048]{2,1,0:T(8,128)(2,1)}, u32[]{:S(2)}) copy-start(bf16[1,128,2048]{2,1,0:T(8,128)(2,1)} %param.6) | copy-start | bytes 1572868
  53.8 25.9 %copy-start.1 = (bf16[1,128,2048]{2,1,0:T(8,128)(2,1)S(1)}, bf16[1,128,2048]{2,1,0:T(8,128)(2,1)}, u32[]{:S(2)}) copy-start(bf16[1,128,2048]{2,1,0:T(8,128)(2,1)} %param.7) | copy-start | bytes 1572868
